TPU v7x, 128 devices: a whole 4x4x4 slice. The times are simulated.
128 devices in a mesh: lat: 4 (over y_hi, core), lon: 32 (over x, z, y_lo).
Axes of the slice: x: 4, y: 4 (y_hi: 2, y_lo: 2; y = y_hi * 2 + y_lo), z: 4, core: 2. Of those that a mesh axis runs over, the one named last changes fastest.
Arguments:
- node_latents: bfloat16 [8, 96, 64, 512], P('lat', 'lon'), may hold values from -6 to 6
- edge_latents: bfloat16 [4, 32, 3072, 512], P('lat', 'lon'), may hold values from -6 to 6
- senders: int32 [4, 32, 3072], P('lat', 'lon'), may hold values from 0 to 3327, as said below
- receivers: int32 [4, 32, 3072], P('lat', 'lon'), may hold values from 0 to 383
- edge_count: int32 [4, 32], P('lat', 'lon'), may hold values from 1536 to 3072, as said below
- edge_self_w: bfloat16 [512, 512], replicated, may hold values from -0.25 to 0.25
- edge_send_w: bfloat16 [512, 512], replicated, may hold values from -0.25 to 0.25
- edge_recv_w: bfloat16 [512, 512], replicated, may hold values from -0.25 to 0.25
- edge_out_w: bfloat16 [512, 512], replicated, may hold values from -0.25 to 0.25
- node_self_w: bfloat16 [512, 512], replicated, may hold values from -0.25 to 0.25
- node_aggr_w: bfloat16 [512, 512], replicated, may hold values from -0.25 to 0.25
- node_out_w: bfloat16 [512, 512], replicated, may hold values from -0.25 to 0.25
- edge_gain: float32 [512], replicated, may hold values from 0.1 to 1.9
- node_gain: float32 [512], replicated, may hold values from 0.1 to 1.9
- node_upstream: bfloat16 [8, 96, 64, 512], P('lat', 'lon'), may hold values from -6 to 6
- edge_upstream: bfloat16 [4, 32, 3072, 512], P('lat', 'lon'), may hold values from -6 to 6
Outputs:
- node_update: bfloat16 [8, 96, 64, 512], P('lat', 'lon')
- edge_update: bfloat16 [4, 32, 3072, 512], P('lat', 'lon')
- node_grads: float32 [8, 96, 64, 512], P('lat', 'lon')
- edge_grads: float32 [4, 32, 3072, 512], P('lat', 'lon')
Inputs may be any that keep to these rules, and one draw needn't show every extreme that they name: A sender below 1280 lies in the receiver's block or one of the eight blocks around it, never in a block row outside the grid; a sender of 1280 or more names coarse node senders - 1280. Exactly 768 slots of each tile name coarse nodes, and at most 6 slots of one tile name coarse nodes of any one tile. `edge_count`: the tiles of the first and last latitude band have all 3072 slots live.
All inputs are finite; a program needn't handle non-finite values.
Results may differ from a plain program's by a relative error of at most 0.013.
Values may be sent and summed in bfloat16 or wider, within the bound.
A program may use at most 192 MiB of HBM per device.

v0:
```python
import jax
import jax.numpy as jnp
from jax import lax
from jax.sharding import PartitionSpec as P

COARSE_DEV = 16


EPSILON = 1e-05


def with_halo(shard, sides, width, wrap):
    for axis, dim in sides:
        size, length = (lax.axis_size(axis), shard.shape[dim])
        up = [(i, (i + 1) % size) for i in range(size if wrap else size - 1)]
        down = [(j, i) for i, j in up]
        last = lax.slice_in_dim(shard, length - width, length, axis=dim)
        initial = lax.slice_in_dim(shard, 0, width, axis=dim)
        before = lax.ppermute(last, axis, up)
        after = lax.ppermute(initial, axis, down)
        shard = jnp.concatenate([before, shard, after], axis=dim)
    return shard


def from_behind(shard, axis, by):
    size = lax.axis_size(axis)
    pairs = [(i, i + by) for i in range(size) if 0 <= i + by < size]
    return lax.ppermute(shard, axis, pairs)


def passed_along(value, axis, steps):
    count = lax.axis_size(axis)
    pairs = [(source, (source + steps) % count) for source in range(count)]
    return lax.ppermute(value, axis, pairs)


def matmul(left, right):
    return jnp.dot(left, right, preferred_element_type=jnp.float32)


def layer_norm(hidden):
    center = hidden - jnp.mean(hidden, -1, keepdims=True)
    inv_std = lax.rsqrt(jnp.mean(center * center, -1, keepdims=True) + EPSILON)
    return (center * inv_std, inv_std)


def norm_back(grad_out, normed, inv_std):
    mean_grad = jnp.mean(grad_out, -1, keepdims=True)
    mean_cross = jnp.mean(grad_out * normed, -1, keepdims=True)
    return inv_std * (grad_out - mean_grad - normed * mean_cross)


def silu_grad(pre_act):
    sigmoid = jax.nn.sigmoid(pre_act)
    return sigmoid * (1.0 + pre_act * (1.0 - sigmoid))


def local_pass(
    edge_rows,
    sender_term,
    recv_rows,
    live_mask,
    flat_nodes,
    receiver_ids,
    up_nodes,
    up_edges,
    weights,
    gains,
):
    self_w, recv_w, out_w, node_w, aggr_w, node_out = weights
    edge_gain, node_gain = gains
    edge_pre = matmul(edge_rows, self_w) + sender_term + matmul(recv_rows, recv_w)
    edge_act = jax.nn.silu(edge_pre).astype(jnp.bfloat16)
    edge_normed, edge_rstd = layer_norm(matmul(edge_act, out_w))
    message = (live_mask * edge_normed * edge_gain).astype(jnp.bfloat16)
    edge_new = (edge_rows.astype(jnp.float32) + message.astype(jnp.float32)).astype(jnp.bfloat16)
    aggregate = (
        jnp.zeros(flat_nodes.shape, jnp.float32)
        .at[receiver_ids]
        .add(message.astype(jnp.float32))
        .astype(jnp.bfloat16)
    )
    node_pre = matmul(flat_nodes, node_w) + matmul(aggregate, aggr_w)
    node_act = jax.nn.silu(node_pre).astype(jnp.bfloat16)
    node_normed, node_rstd = layer_norm(matmul(node_act, node_out))
    node_new = (flat_nodes.astype(jnp.float32) + node_normed * node_gain).astype(jnp.bfloat16)
    up_node32 = up_nodes.astype(jnp.float32)
    up_edge32 = up_edges.astype(jnp.float32)
    node_hidden_grad = norm_back(up_node32 * node_gain, node_normed, node_rstd).astype(jnp.bfloat16)
    node_pre_grad = (matmul(node_hidden_grad, node_out.T) * silu_grad(node_pre)).astype(
        jnp.bfloat16
    )
    node_grad = up_node32 + matmul(node_pre_grad, node_w.T)
    aggregate_grad = matmul(node_pre_grad, aggr_w.T)
    message_grad = live_mask * (up_edge32 + aggregate_grad[receiver_ids])
    edge_hidden_grad = norm_back(message_grad * edge_gain, edge_normed, edge_rstd).astype(
        jnp.bfloat16
    )
    pre_grad = (matmul(edge_hidden_grad, out_w.T) * silu_grad(edge_pre)).astype(jnp.bfloat16)
    edge_grad = up_edge32 + matmul(pre_grad, self_w.T)
    node_grad = node_grad.at[receiver_ids].add(matmul(pre_grad, recv_w.T))
    return (edge_new, node_new, edge_grad, node_grad, pre_grad)


def body(
    node_latents,
    edge_latents,
    senders,
    receivers,
    edge_count,
    edge_self_w,
    edge_send_w,
    edge_recv_w,
    edge_out_w,
    node_self_w,
    node_aggr_w,
    node_out_w,
    edge_gain,
    node_gain,
    node_upstream,
    edge_upstream,
):
    rows_lat, rows_lon, block_size, feature = node_latents.shape
    slot_count = edge_latents.shape[2]
    flat_nodes = node_latents.reshape(-1, feature)
    edge_rows = edge_latents.reshape(slot_count, feature)
    sender_ids = senders.reshape(slot_count)
    receiver_ids = receivers.reshape(slot_count)
    live_mask = (jnp.arange(slot_count) < edge_count[0, 0]).astype(jnp.float32)[:, None]
    recv_rows = flat_nodes[receiver_ids]
    lon_wide = with_halo(node_latents, (("lon", 1),), 1, True)
    extended = with_halo(lon_wide, (("lat", 0),), 1, False)
    far_rows = lax.all_gather(node_latents[0:1, 0, :COARSE_DEV], ("lat", "lon"), axis=0, tiled=True)
    sender_table = jnp.concatenate(
        [extended.reshape(-1, feature), far_rows.reshape(-1, feature)], 0
    )
    sender_term = matmul(sender_table[sender_ids], edge_send_w)
    ext_rows = (rows_lat + 2) * (rows_lon + 2) * block_size
    weights = (edge_self_w, edge_recv_w, edge_out_w, node_self_w, node_aggr_w, node_out_w)
    gains = (edge_gain, node_gain)
    up_nodes = node_upstream.reshape(-1, feature)
    up_edges = edge_upstream.reshape(slot_count, feature)
    edge_new, node_new, edge_grad, node_grad, pre_grad = local_pass(
        edge_rows,
        sender_term,
        recv_rows,
        live_mask,
        flat_nodes,
        receiver_ids,
        up_nodes,
        up_edges,
        weights,
        gains,
    )
    sender_grad = matmul(pre_grad, edge_send_w.T)
    table_grad = (
        jnp.zeros((sender_table.shape[0], feature), jnp.float32).at[sender_ids].add(sender_grad)
    )
    rim_grad = table_grad[:ext_rows].reshape(rows_lat + 2, rows_lon + 2, block_size, feature)
    from_next = from_behind(rim_grad[0].astype(jnp.bfloat16), "lat", -1).astype(jnp.float32)
    from_prev = from_behind(rim_grad[-1].astype(jnp.bfloat16), "lat", 1).astype(jnp.float32)
    inner_grad = rim_grad[1:-1]
    inner_grad = inner_grad.at[-1].add(from_next).at[0].add(from_prev)
    from_east = passed_along(inner_grad[:, 0].astype(jnp.bfloat16), "lon", -1).astype(jnp.float32)
    from_west = passed_along(inner_grad[:, -1].astype(jnp.bfloat16), "lon", 1).astype(jnp.float32)
    core_grad = inner_grad[:, 1:-1].at[:, -1].add(from_east).at[:, 0].add(from_west)
    far_grad = table_grad[ext_rows:].reshape(-1, COARSE_DEV, feature)
    owned_grad = lax.psum_scatter(far_grad, ("lat", "lon"), scatter_dimension=0, tiled=True)
    core_grad = core_grad.at[0, 0, :COARSE_DEV].add(owned_grad[0])
    returned = core_grad.reshape(-1, feature)
    node_grads = (node_grad + returned).reshape(rows_lat, rows_lon, block_size, feature)
    node_update = node_new.reshape(rows_lat, rows_lon, block_size, feature)
    edge_update = edge_new.reshape(1, 1, slot_count, feature)
    edge_grads = edge_grad.reshape(1, 1, slot_count, feature)
    return (node_update, edge_update, node_grads, edge_grads)


def solution(mesh):
    return jax.shard_map(
        body,
        mesh=mesh,
        in_specs=(
            P("lat", "lon", None, None),
            P("lat", "lon", None, None),
            P("lat", "lon", None),
            P("lat", "lon", None),
            P("lat", "lon"),
            P(),
            P(),
            P(),
            P(),
            P(),
            P(),
            P(),
            P(),
            P(),
            P("lat", "lon", None, None),
            P("lat", "lon", None, None),
        ),
        out_specs=(
            P("lat", "lon", None, None),
            P("lat", "lon", None, None),
            P("lat", "lon", None, None),
            P("lat", "lon", None, None),
        ),
        check_vma=False,
    )
```

profile of v0, /device:TPU:0, one launch (start us, length us, event | category | flops | bytes accessed | tf_op | source)
XLA Modules:
  0.0 1127.7 jit_solution(11644854197600881498)
XLA Ops:
  7.2 1.4 slice.196
  8.7 1.0 fusion.32
  9.7 1.7 collective-permute-start
  11.4 5.8 collective-permute-start.1
  17.2 4.6 copy.40
  22.5 0.2 multiply_reduce_fusion.3
  22.7 0.6 div.43
  23.3 4.7 copy.42
  28.0 13.2 %gather_fusion.1 = bf16[3072,512]{1,0:T(8,128)(2,1)} fusion(bf16[384,512]{1,0:T(8,128)(2,1)S(1)} %bitcast.97, s32[3072]{0:T(1024)S(1)} %broadcast_clamp_fusion), kind=kCustom, calls=%fused_computation.1 | custom fusion | bytes 6303744 | tf_op jit(solution)/shard_map/gather | solution.py:130
  41.3 6.5 fusion.7
  47.9 1.3 collective-permute-start.3
  49.2 3.5 collective-permute-start.2
  52.8 1.2 fusion.35
  54.0 0.2 pad_maximum_fusion.1
  54.2 256.6 %all-gather.3.cloned.1.call-done = bf16[128,1,16,512]{3,2,1,0:T(8,128)(2,1)} async-done(((bf16[1,1,16,512]{3,2,1,0:T(8,128)(2,1)}), bf16[128,1,16,512]{3,2,1,0:T(8,128)(2,1)}) %all-gather.3.cloned.1.call-update) | async-done | bytes 2097168 | tf_op jit(solution)/shard_map/all_gather | solution.py:133
  310.8 3.5 pad_maximum_fusion
  314.3 15.8 %gather_fusion = bf16[3072,512]{1,0:T(8,128)(2,1)} fusion(bf16[3328,512]{1,0:T(8,128)(2,1)} %pad_maximum_fusion, s32[3072]{0:T(1024)S(1)} %broadcast_clamp_fusion.1), kind=kCustom, calls=%fused_computation | custom fusion | bytes 6303744 | tf_op jit(solution)/shard_map/gather | solution.py:137
  330.1 3.8 fusion.36
  334.0 4.7 add_add_fusion
  338.8 2.4 fusion.33
  341.2 0.2 copy-done.11
  341.4 0.8 multiply_reduce_fusion.1
  342.2 3.4 copy-done.12
  345.6 5.5 fusion.6
  351.1 6.6 copy.41
  357.7 19.6 %scatter_custom_fusion = f32[384,512]{1,0:T(8,128)S(1)} fusion(s32[3072]{0:T(1024)S(1)} %bitcast.112, f32[3072,512]{1,0:T(8,128)} %copy.41, f32[]{:T(128)} %constant.159.clone.1), kind=kCustom, calls=%fused_computation.52 | custom fusion | flops 1572864 | bytes 786944 | tf_op jit(solution)/shard_map/scatter-add | solution.py:80
  377.3 1.5 convolution_add_fusion.1
  378.8 1.6 fusion.34
  380.4 0.2 multiply_reduce_fusion.4
  380.7 0.3 multiply_reduce_fusion.2
  381.0 1.1 multiply_convert_fusion.6
  382.1 0.5 fusion.15
  382.6 0.4 fusion.37
  383.0 0.3 copy-done.23
  383.4 12.8 %gather_fusion.2 = f32[3072,512]{1,0:T(8,128)} fusion(f32[384,512]{1,0:T(8,128)S(1)} %fusion.37, s32[3072]{0:T(1024)S(1)} %broadcast_clamp_fusion), kind=kCustom, calls=%fused_computation.2 | custom fusion | bytes 12595200 | tf_op jit(solution)/shard_map/gather | solution.py:95
  396.2 6.7 copy.43
  402.9 7.2 fusion.28
  410.1 0.5 copy-done.7
  410.6 1.8 copy-done.10
  412.4 7.1 multiply_convert_fusion
  419.5 1.7 copy-done.5
  421.2 4.7 fusion.38
  425.9 22.6 %scatter_custom_fusion.1 = f32[3328,512]{1,0:T(8,128)} fusion(s32[3072]{0:T(1024)} %bitcast.115, f32[3072,512]{1,0:T(8,128)} %fusion.38, f32[]{:T(128)} %constant.159.clone.1), kind=kCustom, calls=%fused_computation.22 | custom fusion | flops 1572864 | bytes 6816256 | tf_op jit(solution)/shard_map/scatter-add | solution.py:157
  448.5 4.6 slice.229
  453.1 3.5 convert.19
  456.7 1.4 collective-permute-start.4
  458.1 3.7 collective-permute-start.5
  461.9 4.6 fusion.2
  466.5 0.1 bitcast_dynamic-update-slice_fusion
  466.6 0.2 fusion.16
  466.7 0.1 convert.21
  466.8 0.7 slice_bitcast_fusion.1
  467.6 4.7 collective-permute-start.6
  472.3 4.6 fusion.39
  476.9 4.6 copy.49
  481.5 6.6 copy.50
  488.2 0.1 copy.52
  488.4 9.7 collective-permute-done.7
  498.1 0.1 constant_dynamic-update-slice_fusion.3
  498.2 600.7 %reduce-scatter.2.cloned.1.call-done = f32[1,16,512]{2,1,0:T(8,128)} async-done(((f32[128,16,512]{2,1,0:T(8,128)}), f32[1,16,512]{2,1,0:T(8,128)}) %reduce-scatter.2.cloned.1.call-update) | async-done | bytes 32784 | tf_op jit(solution)/shard_map/reduce_scatter | solution.py:168
  1098.9 0.8 fusion.23
  1099.7 0.4 fusion.14
  1100.2 19.5 %scatter_fusion = f32[384,512]{1,0:T(8,128)S(1)} fusion(f32[384,512]{1,0:T(8,128)S(1)} %fusion.14, s32[3072]{0:T(1024)S(1)} %bitcast.113, f32[3072,512]{1,0:T(8,128)} %fusion.39), kind=kCustom, calls=%fused_computation.5 | custom fusion | flops 1572864 | bytes 18886656 | tf_op jit(solution)/shard_map/scatter-add | solution.py:101
  1119.7 0.9 copy-done.2
  (110 shorter events, 0.8 us)
Async XLA Ops:
  7.2 331.6 %copy-start = (bf16[512,512]{1,0:T(8,128)(2,1)S(1)}, bf16[512,512]{1,0:T(8,128)(2,1)}, u32[]{:S(2)}) copy-start(bf16[512,512]{1,0:T(8,128)(2,1)} %param.34) | copy-start | bytes 1572868
  7.2 15.3 %copy-start.13 = (bf16[2,3,64,512]{3,2,1,0:T(8,128)(2,1)S(1)}, bf16[2,3,64,512]{3,2,1,0:T(8,128)(2,1)}, u32[]{:S(2)}) copy-start(bf16[2,3,64,512]{3,2,1,0:T(8,128)(2,1)} %param.40) | copy-start | bytes 1179652
  7.2 15.3 %copy-start.32 = (f32[512]{0:T(512)S(1)}, f32[512]{0:T(512)}, u32[]{:S(2)}) copy-start(f32[512]{0:T(512)} %param.39) | copy-start | bytes 6148
  7.2 303.6 %all-gather.3.cloned.1.call-start = ((), (), s32[]{:S(2)}) async-start(), calls=%async_computation.2 | async-start | bytes 2113536 | tf_op jit(solution)/shard_map/all_gather | solution.py:133
  8.7 1090.2 %reduce-scatter.2.cloned.1.call-start = ((), (), s32[]{:S(2)}) async-start(), calls=%async_computation.1 | async-start | bytes 4227072 | tf_op jit(solution)/shard_map/reduce_scatter | solution.py:168
  9.7 38.1 %collective-permute-start = (bf16[2,1,64,512]{3,2,1,0:T(8,128)(2,1)S(1)}, bf16[2,1,64,512]{3,2,1,0:T(8,128)(2,1)S(1)}, u32[]{:S(2)}, u32[]{:S(2)}) collective-permute-start(bf16[2,1,64,512]{3,2,1,0:T(8,128)(2,1)S(1)} %get-tuple-element.91), channel_id=1, source_target_pairs={{0,1},{1,2},{2,3},{3,4},{4,5},{5,6},{6,7},{7,8},{8,9},{9,10},{10,1... | collective-permute-start | bytes 393224 | tf_op jit(solution)/shard_map/ppermute | solution.py:19
  11.4 16.5 %copy-start.33 = (s32[1,1,3072]{2,1,0:T(1,128)S(1)}, s32[1,1,3072]{2,1,0:T(1,128)}, u32[]{:S(2)}) copy-start(s32[1,1,3072]{2,1,0:T(1,128)} %param.29) | copy-start | bytes 36868
  11.4 16.6 %copy-start.3 = (bf16[2,3,64,512]{3,2,1,0:T(8,128)(2,1)S(1)}, bf16[2,3,64,512]{3,2,1,0:T(8,128)(2,1)}, u32[]{:S(2)}) copy-start(bf16[2,3,64,512]{3,2,1,0:T(8,128)(2,1)} %param.26) | copy-start | bytes 1179652
  11.4 36.4 %collective-permute-start.1 = (bf16[2,1,64,512]{3,2,1,0:T(8,128)(2,1)S(1)}, bf16[2,1,64,512]{3,2,1,0:T(8,128)(2,1)S(1)}, u32[]{:S(2)}, u32[]{:S(2)}) collective-permute-start(bf16[2,1,64,512]{3,2,1,0:T(8,128)(2,1)S(1)} %get-tuple-element.90), channel_id=1, source_target_pairs={{1,0},{2,1},{3,2},{4,3},{5,4},{6,5},{7,6},{8,7},{9,8},{10,9},{11,1... | collective-permute-start | bytes 393224 | tf_op jit(solution)/shard_map/ppermute | solution.py:20
  28.0 329.7 %copy-start.29 = (s32[3072,1]{0,1:T(1,128)}, s32[3072,1]{0,1:T(1,128)S(1)}, u32[]{:S(2)}) copy-start(s32[3072,1]{0,1:T(1,128)S(1)} %compare_select_fusion.1) | copy-start | bytes 36868
  28.0 13.2 %copy-start.15 = (bf16[512,512]{1,0:T(8,128)(2,1)S(1)}, bf16[512,512]{1,0:T(8,128)(2,1)}, u32[]{:S(2)}) copy-start(bf16[512,512]{1,0:T(8,128)(2,1)} %param.31) | copy-start | bytes 1572868
  41.3 6.5 copy-start.34
  41.3 11.5 %copy-start.17 = (bf16[512,512]{1,0:T(8,128)(2,1)S(1)}, bf16[512,512]{1,0:T(8,128)(2,1)}, u32[]{:S(2)}) copy-start(bf16[512,512]{1,0:T(8,128)(2,1)} %param.35) | copy-start | bytes 1572868
  47.8 266.6 %copy-start.31 = (s32[3072,1]{0,1:T(1,128)}, s32[3072,1]{0,1:T(1,128)S(1)}, u32[]{:S(2)}) copy-start(s32[3072,1]{0,1:T(1,128)S(1)} %compare_select_fusion) | copy-start | bytes 36868
  47.9 6.1 collective-permute-start.3
  49.2 4.8 collective-permute-start.2
  52.8 289.4 %copy-start.25 = (f32[3072]{0:T(1024)}, f32[3072]{0:T(1024)S(1)}, u32[]{:S(2)}) copy-start(f32[3072]{0:T(1024)S(1)} %fusion.24) | copy-start | bytes 36868
  314.3 15.8 %copy-start.19 = (bf16[512,512]{1,0:T(8,128)(2,1)S(1)}, bf16[512,512]{1,0:T(8,128)(2,1)}, u32[]{:S(2)}) copy-start(bf16[512,512]{1,0:T(8,128)(2,1)} %param.32) | copy-start | bytes 1572868
  330.1 3.8 copy-start.9
  330.1 3.9 copy-start.21
  338.8 2.6 copy-start.11
  341.4 9.7 copy-start.4
  341.4 4.2 copy-start.12
  341.4 4.2 copy-start.35
  345.6 5.5 copy-start.27
  351.1 26.2 %copy-start.14 = (f32[384,512]{1,0:T(8,128)S(1)}, f32[384,512]{1,0:T(8,128)}, u32[]{:S(2)}) copy-start(f32[384,512]{1,0:T(8,128)} %fusion.35) | copy-start | bytes 2359300
  357.7 23.2 %copy-start.36 = (f32[384]{0:T(512)S(1)}, f32[384]{0:T(512)}, u32[]{:S(2)}) copy-start(f32[384]{0:T(512)} %div.43) | copy-start | bytes 4612
  377.3 4.8 copy-start.37
  378.8 3.8 copy-start.16
  382.6 0.7 copy-start.23
  396.2 13.9 %slice-start.2 = ((s8[6291456]{0:T(1024)(128)(4,1)}), s8[2097152]{0:T(1024)(128)(4,1)S(1)}, s32[]{:S(2)}) async-start(s8[6291456]{0:T(1024)(128)(4,1)} %bitcast.101), calls=%async_computation.5 | async-start | bytes 4194304
  402.9 7.2 slice-start.3
  402.9 7.7 copy-start.7
  402.9 9.5 copy-start.10
  402.9 9.5 copy-start.26
  402.9 9.5 copy-start.28
  412.4 8.8 copy-start.20
  419.5 1.7 copy-start.5
  453.0 8.8 copy-start.6
  453.1 8.8 copy-start.8
  456.7 9.8 collective-permute-start.4
  458.1 8.4 slice-start
  458.1 8.4 slice-start.1
  458.1 8.5 collective-permute-start.5
  466.5 5.8 copy-start.22
  467.6 20.8 %collective-permute-start.6 = (bf16[2,64,512]{2,1,0:T(8,128)(2,1)}, bf16[2,64,512]{2,1,0:T(8,128)(2,1)S(1)}, u32[]{:S(2)}, u32[]{:S(2)}) collective-permute-start(bf16[2,64,512]{2,1,0:T(8,128)(2,1)} %get-tuple-element.87), channel_id=1, source_target_pairs={{0,31},{1,0},{2,1},{3,2},{4,3},{5,4},{6,5},{7,6},{8,7},{9,8},{10,9... | collective-permute-start | bytes 393224 | tf_op jit(solution)/shard_map/ppermute | solution.py:34
  488.1 611.7 %copy-start.18 = (bf16[512,512]{1,0:T(8,128)(2,1)S(1)}, bf16[512,512]{1,0:T(8,128)(2,1)}, u32[]{:S(2)}) copy-start(bf16[512,512]{1,0:T(8,128)(2,1)} %param.35) | copy-start | bytes 1572868
  488.1 611.7 %copy-start.24 = (bf16[384,512]{1,0:T(8,128)(2,1)S(1)}, bf16[384,512]{1,0:T(8,128)(2,1)}, u32[]{:S(2)}) copy-start(bf16[384,512]{1,0:T(8,128)(2,1)} %copy-done.23) | copy-start | bytes 1179652
  488.1 612.1 %copy-start.30 = (s32[3072,1]{0,1:T(1,128)S(1)}, s32[3072,1]{0,1:T(1,128)}, u32[]{:S(2)}) copy-start(s32[3072,1]{0,1:T(1,128)} %copy-done.29) | copy-start | bytes 36868
  488.2 9.9 collective-permute-start.7
  1100.2 20.4 %copy-start.1 = (bf16[512,512]{1,0:T(8,128)(2,1)S(1)}, bf16[512,512]{1,0:T(8,128)(2,1)}, u32[]{:S(2)}) copy-start(bf16[512,512]{1,0:T(8,128)(2,1)} %param.34) | copy-start | bytes 1572868
  1119.7 0.9 copy-start.2
Sparse Core Ops, SparseCore 0:
  10.3 300.4 all-gather.2
  453.2 645.6 reduce-scatter.1
where the time goes:
time: 1130 us
  waiting for transfers between devices  867 us (77%)
  local copies, waits for them, and re-layouts  93.2 us (8%)
  other arithmetic  85.5 us (8%)
  matrix products  44 us (4%)
  starting transfers between devices  22.3 us (2%)
  between operations  15.6 us (1%)
    reduce_scatter x1, waiting for transfers between devices, body(): lax.psum_scatter(far_grad, ('lat', 'lon'), scatter_dimension=0, tiled=True)  601 us
    all_gather x1, waiting for transfers between devices, body(): lax.all_gather(node_latents[0:1, 0, :COARSE_DEV], ('lat', 'lon'), axis=0,...  257 us
    dot_general x14, matrix products, matmul(): return jnp.dot(left, right, preferred_element_type=jnp.float32)  44 us
    unnamed x87, local copies, waits for them, and re-layouts  29.5 us
  transfers between devices with their start and end apart: 10, of which 3 were waited for; matrix products, arithmetic and copies ran while one was open for 5% of the time, Pallas kernels for 0%

commit v1 on v0

v1 whole, which is shorter than its diff:
```python
import jax
import jax.numpy as jnp
from jax import lax
from jax.experimental import pallas as pl
from jax.experimental.pallas import tpu as pltpu
from jax.sharding import PartitionSpec as P

MESH = pl.DeviceIdType.MESH
F32 = jnp.float32
BF16 = jnp.bfloat16
EPSILON = 1e-05

D = 512
BLOCK = 64
SLOTS = 3072
NODES = 384
EXT = 1280
OWNERS = 128
MEMBERS = 16
COARSE = OWNERS * MEMBERS
PER_OWNER = 8
PACKED = OWNERS * PER_OWNER
RECV_AT = EXT + PACKED
TABLE = RECV_AT + NODES
STEP = 256
STEPS = SLOTS // STEP
LANES = 128
GROUP = 16
GROUPS = OWNERS // GROUP
LONS = 32
CHUNK = 8
VMEM_BYTES = 60 * 1024 * 1024


def dot(left, right):
    return jnp.dot(left, right, preferred_element_type=F32)


def dot_t(left, right):
    return lax.dot_general(left, right, (((1,), (1,)), ((), ())), preferred_element_type=F32)


def t_dot(left, right):
    return lax.dot_general(left, right, (((0,), (0,)), ((), ())), preferred_element_type=F32)


def onehot(mask):
    return jnp.where(mask, 1.0, 0.0).astype(BF16)


def mean(rows):
    return jnp.sum(rows, -1, keepdims=True) * (1.0 / D)


def sigmoid(pre):
    return 0.5 * jnp.tanh(0.5 * pre) + 0.5


def places():
    lat = lax.axis_index("lat")
    lon = lax.axis_index("lon")
    return lat, lon, lat % 2, lat // 2


def shifted(lat, lon, row, col):
    return {"lat": lax.rem(lat + row + 4, 4), "lon": lax.rem(lon + col + LONS, LONS)}


def greet(lat, lon, core, half):
    barrier = pltpu.get_barrier_semaphore()
    for row in (-1, 1):
        for col in (-1, 0, 1):
            pl.semaphore_signal(barrier, inc=1, device_id=shifted(lat, lon, row, col), device_id_type=MESH)

    def one(step, carry):
        peer = {
            "lat": lax.rem(half + step // LONS, 2) * 2 + core,
            "lon": lax.rem(lon + step, LONS),
        }
        pl.semaphore_signal(barrier, inc=1, device_id=peer, device_id_type=MESH)
        return carry

    lax.fori_loop(1, 2 * LONS, one, 0)
    pl.semaphore_wait(barrier, 6 + 2 * LONS - 1)


HALO = (
    ((-1, 0), (0, 1), (0, 3), (3, 1), (1, 3)),
    ((1, 0), (1, 1), (0, 3), (0, 1), (1, 3)),
    ((0, -1), (0, 2), (0, 1), (1, 2), (4, 1)),
    ((0, 1), (0, 2), (2, 1), (1, 2), (0, 1)),
    ((-1, -1), (0, 1), (0, 1), (3, 1), (4, 1)),
    ((-1, 1), (0, 1), (2, 1), (3, 1), (0, 1)),
    ((1, -1), (1, 1), (0, 1), (0, 1), (4, 1)),
    ((1, 1), (1, 1), (2, 1), (0, 1), (0, 1)),
)


def spread_kernel(nodes, ext, coarse, own_sem, halo_send, halo_recv, far_send, far_recv, pass_send, pass_recv):
    lat, lon, core, half = places()
    greet(lat, lon, core, half)
    mine = lat * LONS + lon
    first = nodes.at[0, 0, pl.ds(0, MEMBERS)]

    own = pltpu.make_async_copy(nodes, ext.at[pl.ds(1, 2), pl.ds(1, 3)], own_sem)
    own.start()
    kept = pltpu.make_async_copy(first, coarse.at[mine], far_recv.at[half, lon // CHUNK])
    kept.start()

    def far_copy(step):
        peer = {
            "lat": lax.rem(half + step // LONS, 2) * 2 + core,
            "lon": lax.rem(lon + step, LONS),
        }
        return pltpu.make_async_remote_copy(
            src_ref=first,
            dst_ref=coarse.at[mine],
            send_sem=far_send,
            recv_sem=far_recv.at[half, lon // CHUNK],
            device_id=peer,
            device_id_type=MESH,
        )

    def far_one(step, carry):
        far_copy(step).start()
        return carry

    lax.fori_loop(1, 2 * LONS, far_one, 0)

    halos = []
    for at, ((row, col), (r0, rn), (c0, cn), (er, ern), (ec, ecn)) in enumerate(HALO):
        copy = pltpu.make_async_remote_copy(
            src_ref=nodes.at[pl.ds(r0, rn), pl.ds(c0, cn)],
            dst_ref=ext.at[pl.ds(er, ern), pl.ds(ec, ecn)],
            send_sem=halo_send.at[at],
            recv_sem=halo_recv.at[at],
            device_id=shifted(lat, lon, row, col),
            device_id_type=MESH,
        )
        copy.start()
        halos.append(copy)

    partner = {"lat": half * 2 + 1 - core, "lon": lon}
    passes = []
    for far in range(2):
        for part in range(LONS // CHUNK):
            at = (far * 2 + core) * LONS + part * CHUNK
            block = coarse.at[pl.ds(at, CHUNK)]
            pltpu.make_async_copy(block, block, far_recv.at[far, part]).wait()
            copy = pltpu.make_async_remote_copy(
                src_ref=block,
                dst_ref=block,
                send_sem=pass_send.at[far, part],
                recv_sem=pass_recv.at[far, part],
                device_id=partner,
                device_id_type=MESH,
            )
            copy.start()
            passes.append(copy)
    own.wait()
    for copy in halos:
        copy.wait()
    for copy in passes:
        copy.wait()
    sent = coarse.at[pl.ds(0, 2 * LONS - 1)]
    pltpu.make_async_copy(sent, sent, far_send).wait()


def spread(nodes):
    return pl.pallas_call(
        spread_kernel,
        out_shape=(
            jax.ShapeDtypeStruct((4, 5, BLOCK, D), BF16),
            jax.ShapeDtypeStruct((OWNERS, MEMBERS, D), BF16),
        ),
        in_specs=[pl.BlockSpec(memory_space=pl.ANY)],
        out_specs=(pl.BlockSpec(memory_space=pl.ANY),) * 2,
        scratch_shapes=[
            pltpu.SemaphoreType.DMA,
            pltpu.SemaphoreType.DMA((8,)),
            pltpu.SemaphoreType.DMA((8,)),
            pltpu.SemaphoreType.DMA,
            pltpu.SemaphoreType.DMA((2, LONS // CHUNK)),
            pltpu.SemaphoreType.DMA((2, LONS // CHUNK)),
            pltpu.SemaphoreType.DMA((2, LONS // CHUNK)),
        ],
        compiler_params=pltpu.CompilerParams(collective_id=0, has_side_effects=True),
        name="spread",
    )(nodes)


BACK = (
    ((-1, 0), (0, 1), (1, 3)),
    ((1, 0), (3, 1), (1, 3)),
    ((0, -1), (1, 2), (0, 1)),
    ((0, 1), (1, 2), (4, 1)),
    ((-1, -1), (0, 1), (0, 1)),
    ((-1, 1), (0, 1), (4, 1)),
    ((1, -1), (3, 1), (0, 1)),
    ((1, 1), (3, 1), (4, 1)),
)


def collect_kernel(
    rim, far_grad, part, send_w, out,
    paired, summed, landed, rows_in, cols_in, corners_in, total,
    halo_send, halo_recv, pair_send, pair_recv, far_send, far_recv,
):
    lat, lon, core, half = places()
    greet(lat, lon, core, half)
    mine = half * LONS + lon
    partner = {"lat": half * 2 + 1 - core, "lon": lon}
    parts = LONS // CHUNK

    pairs = []
    for hop in range(2):
        for step in range(parts):
            far = lax.rem(half + hop, 2)
            group = lax.rem(lon // CHUNK + step, parts)
            at = (far * 2 + 1 - core) * LONS + group * CHUNK
            copy = pltpu.make_async_remote_copy(
                src_ref=far_grad.at[pl.ds(at, CHUNK)],
                dst_ref=paired.at[hop, step],
                send_sem=pair_send.at[hop, step],
                recv_sem=pair_recv.at[hop, step],
                device_id=partner,
                device_id_type=MESH,
            )
            copy.start()
            pairs.append((copy, hop, step, far, group))

    targets = [
        rows_in.at[pl.ds(1, 1)], rows_in.at[pl.ds(0, 1)],
        cols_in.at[1], cols_in.at[0],
        corners_in.at[3], corners_in.at[2], corners_in.at[1], corners_in.at[0],
    ]
    halos = []
    for at, ((row, col), (er, ern), (ec, ecn)) in enumerate(BACK):
        copy = pltpu.make_async_remote_copy(
            src_ref=rim.at[pl.ds(er, ern), pl.ds(ec, ecn)],
            dst_ref=targets[at],
            send_sem=halo_send.at[at],
            recv_sem=halo_recv.at[at],
            device_id=shifted(lat, lon, row, col),
            device_id_type=MESH,
        )
        copy.start()
        halos.append(copy)

    for copy, hop, step, far, group in pairs:
        copy.wait_recv()
        at = (far * 2 + core) * LONS + group * CHUNK
        summed[hop, step] = (
            far_grad[pl.ds(at, CHUNK)].astype(F32) + paired[hop, step].astype(F32)
        ).astype(BF16)
        for turn in range(CHUNK):
            place = lax.rem(lon + turn, CHUNK)
            to_lon = group * CHUNK + place
            source = summed.at[hop, step, place]

            def stay():
                pltpu.make_async_copy(source, landed.at[mine], far_recv).start()

            def go():
                pltpu.make_async_remote_copy(
                    src_ref=source,
                    dst_ref=landed.at[mine],
                    send_sem=far_send,
                    recv_sem=far_recv,
                    device_id={"lat": far * 2 + core, "lon": to_lon},
                    device_id_type=MESH,
                ).start()

            if hop == 0 and step == 0 and turn == 0:
                stay()
            else:
                go()

    total[...] = rim[1:3, 1:4].astype(F32)
    for copy in halos:
        copy.wait_recv()
    total[...] += rows_in[...].astype(F32)
    total[:, 0] += cols_in[0][:, 0].astype(F32)
    total[:, 2] += cols_in[1][:, 0].astype(F32)
    total[0, 0] += corners_in[0][0, 0].astype(F32)
    total[0, 2] += corners_in[1][0, 0].astype(F32)
    total[1, 0] += corners_in[2][0, 0].astype(F32)
    total[1, 2] += corners_in[3][0, 0].astype(F32)

    pltpu.make_async_copy(landed, landed, far_recv).wait()

    def add(at, acc):
        return acc + landed[at].astype(F32)

    total[0, 0, :MEMBERS] += lax.fori_loop(0, 2 * LONS, add, jnp.zeros((MEMBERS, D), F32))
    for row in range(2):
        for col in range(3):
            at = (row * 3 + col) * BLOCK
            out[at : at + BLOCK] = part[at : at + BLOCK] + dot_t(total[row, col].astype(BF16), send_w[...])

    for copy in halos:
        copy.wait_send()
    for copy, *_ in pairs:
        copy.wait_send()
    sent = landed.at[pl.ds(0, 2 * LONS - 1)]
    pltpu.make_async_copy(sent, sent, far_send).wait()


def collect(rim, far_grad, part, send_w):
    parts = LONS // CHUNK
    vmem = pl.BlockSpec(memory_space=pltpu.VMEM)
    return pl.pallas_call(
        collect_kernel,
        out_shape=jax.ShapeDtypeStruct((NODES, D), F32),
        in_specs=[vmem] * 4,
        out_specs=vmem,
        scratch_shapes=[
            pltpu.VMEM((2, parts, CHUNK, MEMBERS, D), BF16),
            pltpu.VMEM((2, parts, CHUNK, MEMBERS, D), BF16),
            pltpu.VMEM((2 * LONS, MEMBERS, D), BF16),
            pltpu.VMEM((2, 3, BLOCK, D), BF16),
            pltpu.VMEM((2, 2, 1, BLOCK, D), BF16),
            pltpu.VMEM((4, 1, 1, BLOCK, D), BF16),
            pltpu.VMEM((2, 3, BLOCK, D), F32),
            pltpu.SemaphoreType.DMA((8,)),
            pltpu.SemaphoreType.DMA((8,)),
            pltpu.SemaphoreType.DMA((2, parts)),
            pltpu.SemaphoreType.DMA((2, parts)),
            pltpu.SemaphoreType.DMA,
            pltpu.SemaphoreType.DMA,
        ],
        compiler_params=pltpu.CompilerParams(
            collective_id=1, has_side_effects=True, vmem_limit_bytes=VMEM_BYTES
        ),
        name="collect",
    )(rim, far_grad, part, send_w)


def layer_norm(hidden):
    center = hidden - mean(hidden)
    inv_std = lax.rsqrt(mean(center * center) + EPSILON)
    return center * inv_std, inv_std


def norm_back(grad_out, normed, inv_std):
    return inv_std * (grad_out - mean(grad_out) - normed * mean(grad_out * normed))


def layer_kernel(
    count, senders, receivers, ext, coarse, nodes, node_up, edges, edge_up,
    self_w, send_w, recv_w, out_w, node_w, aggr_w, node_out, edge_gain, node_gain,
    node_new, edge_new, node_grad, edge_grad, rim, far_grad,
    edges_v, up_v, new_v, grad_v, table, hot, packed, picks, requests, slot_of, normed_v, slope_v, rstd_v, pre_grad_v, aggr, aggr_grad,
    edges_sem, up_sem, new_sem, grad_sem,
):
    def rows_of(step):
        return pl.ds(pl.multiple_of(step * STEP, STEP), STEP)

    loads = []
    for step in range(STEPS):
        at = pl.ds(step * STEP, STEP)
        pltpu.make_async_copy(edges.at[at], edges_v.at[at], edges_sem.at[step]).start()
    for step in range(STEPS):
        at = pl.ds(step * STEP, STEP)
        pltpu.make_async_copy(edge_up.at[at], up_v.at[at], up_sem.at[step]).start()

    earlier = onehot(
        lax.broadcasted_iota(jnp.int32, (STEP, STEP), 0) < lax.broadcasted_iota(jnp.int32, (STEP, STEP), 1)
    )
    down = lax.broadcasted_iota(jnp.int32, (OWNERS, STEP), 0)
    requests[...] = jnp.zeros_like(requests)

    def rank_step(step, seen):
        at = rows_of(step)
        ids = senders[:, at]
        far = ids - EXT
        owner = jnp.right_shift(far, 4)
        mask = jnp.broadcast_to(owner, (OWNERS, STEP)) == down
        flags = jnp.where(mask, 1.0, 0.0)
        flags_16 = flags.astype(BF16)
        before = dot(flags_16, earlier) + seen
        rank = jnp.sum(flags * before, 0, keepdims=True).astype(jnp.int32)
        slot_of[0:1, at] = jnp.where(far >= 0, EXT + owner * PER_OWNER + rank, ids)
        member = jnp.where(far >= 0, jnp.bitwise_and(far, MEMBERS - 1) + 1, 0).astype(F32)
        chosen = jnp.where(jnp.broadcast_to(rank, (OWNERS, STEP)) == down, jnp.broadcast_to(member, (OWNERS, STEP)), 0.0)
        requests[...] += dot_t(flags_16, chosen.astype(BF16))
        return seen + jnp.sum(flags, 1, keepdims=True)

    lax.fori_loop(0, STEPS, rank_step, jnp.zeros((OWNERS, 1), F32))

    wide = jnp.broadcast_to(requests[...][:, None, :], (OWNERS, PER_OWNER, LANES)).reshape(PACKED, LANES)
    at_row = jnp.bitwise_and(lax.broadcasted_iota(jnp.int32, (PACKED, LANES), 0), PER_OWNER - 1)
    at_lane = lax.broadcasted_iota(jnp.int32, (PACKED, LANES), 1)
    wanted = jnp.sum(jnp.where(at_row == at_lane, wide, 0.0), 1, keepdims=True).astype(jnp.int32)
    span = GROUP * MEMBERS
    rows_in = lax.broadcasted_iota(jnp.int32, (PACKED, span), 0)
    cols_in = lax.broadcasted_iota(jnp.int32, (PACKED, span), 1)
    same = jnp.bitwise_and(jnp.right_shift(rows_in, 3), GROUP - 1) == jnp.right_shift(cols_in, 4)
    named = wanted == jnp.bitwise_and(cols_in, MEMBERS - 1) + 1
    picks[...] = onehot(jnp.logical_and(same, named))

    for at in range(0, EXT, STEP):
        table[at : at + STEP] = dot(ext[at : at + STEP], send_w[...]).astype(BF16)
    for at in range(0, NODES, LANES):
        table[RECV_AT + at : RECV_AT + at + LANES] = dot(nodes[at : at + LANES], recv_w[...]).astype(BF16)
    for group in range(GROUPS):
        at, span = group * GROUP * PER_OWNER, GROUP * MEMBERS
        packed[at : at + LANES] = dot(
            picks[at : at + LANES], coarse[group * span : (group + 1) * span]
        ).astype(BF16)
    for at in range(0, PACKED, STEP):
        table[EXT + at : EXT + at + STEP] = dot(packed[at : at + STEP], send_w[...]).astype(BF16)

    lane = lax.broadcasted_iota(jnp.int32, (STEP, LANES), 1)
    node_row = lax.broadcasted_iota(jnp.int32, (NODES, STEP), 0)
    slot_row = lax.broadcasted_iota(jnp.int32, (STEP, 1), 0)
    aggr[...] = jnp.zeros_like(aggr)

    def column(ids):
        return jnp.transpose(jnp.broadcast_to(ids, (LANES, STEP)))

    def live_of(step):
        return (slot_row + step * STEP < count[0, 0]).astype(F32)

    def forward(step, carry):
        at = rows_of(step)
        from_col = column(slot_of[0:1, at])
        to_col = column(receivers[:, at])
        for base in range(0, RECV_AT, LANES):
            hot[:, base : base + LANES] = onehot(from_col == lane + base)
        for base in range(0, NODES, LANES):
            hot[:, RECV_AT + base : RECV_AT + base + LANES] = onehot(to_col == lane + base)
        pltpu.make_async_copy(edges.at[at], edges_v.at[at], edges_sem.at[step]).wait()
        rows = edges_v[at]
        pre = dot(rows, self_w[...]) + dot(hot[...], table[...])
        gate = sigmoid(pre)
        act = pre * gate
        slope_v[at] = (gate + act * (1.0 - gate)).astype(BF16)
        normed, rstd = layer_norm(dot(act.astype(BF16), out_w[...]))
        normed_v[at] = normed.astype(BF16)
        rstd_v[at] = jnp.broadcast_to(rstd, (STEP, LANES))
        message = (live_of(step) * normed * edge_gain[...]).astype(BF16)
        new_v[at] = (rows.astype(F32) + message.astype(F32)).astype(BF16)
        pltpu.make_async_copy(new_v.at[at], edge_new.at[at], new_sem.at[step]).start()
        to_hot = onehot(jnp.broadcast_to(receivers[:, at], (NODES, STEP)) == node_row)
        aggr[...] += dot(to_hot, message)
        return carry

    lax.fori_loop(0, STEPS, forward, 0)

    node_rows = nodes[...]
    node_pre = dot(node_rows, node_w[...]) + dot(aggr[...].astype(BF16), aggr_w[...])
    gate = sigmoid(node_pre)
    act = node_pre * gate
    slope = gate + act * (1.0 - gate)
    normed, rstd = layer_norm(dot(act.astype(BF16), node_out[...]))
    node_new[...] = (node_rows.astype(F32) + normed * node_gain[...]).astype(BF16)
    up = node_up[...].astype(F32)
    hidden_grad = norm_back(up * node_gain[...], normed, rstd).astype(BF16)
    pre_grad = (dot_t(hidden_grad, node_out[...]) * slope).astype(BF16)
    node_grad[...] = up + dot_t(pre_grad, node_w[...])
    aggr_grad[...] = dot_t(pre_grad, aggr_w[...]).astype(BF16)

    def backward(step, carry):
        at = rows_of(step)
        to_col = column(receivers[:, at])
        for base in range(0, NODES, LANES):
            hot[:, base : base + LANES] = onehot(to_col == lane + base)
        pltpu.make_async_copy(edge_up.at[at], up_v.at[at], up_sem.at[step]).wait()
        upstream = up_v[at].astype(F32)
        grad = live_of(step) * (upstream + dot(hot[:, :NODES], aggr_grad[...])) * edge_gain[...]
        normed = normed_v[at].astype(F32)
        hidden_grad = norm_back(grad, normed, rstd_v[at][:, :1]).astype(BF16)
        pre_grad = (dot_t(hidden_grad, out_w[...]) * slope_v[at].astype(F32)).astype(BF16)
        pre_grad_v[at] = pre_grad
        grad_v[at] = upstream + dot_t(pre_grad, self_w[...])
        pltpu.make_async_copy(grad_v.at[at], edge_grad.at[at], grad_sem.at[step]).start()
        return carry

    lax.fori_loop(0, STEPS, backward, 0)

    def summed(ids, base, size):
        mask = jnp.broadcast_to(ids, (size, SLOTS)) == lax.broadcasted_iota(jnp.int32, (size, SLOTS), 0) + base
        return dot(onehot(mask), pre_grad_v[...])

    def rim_step(step, carry):
        at = rows_of(step)
        rim[at] = summed(slot_of[0:1, :], step * STEP, STEP).astype(BF16)
        return carry

    def far_step(step, carry):
        at = rows_of(step)
        packed[at] = summed(slot_of[0:1, :], EXT + step * STEP, STEP).astype(BF16)
        return carry

    lax.fori_loop(0, EXT // STEP, rim_step, 0)
    lax.fori_loop(0, PACKED // STEP, far_step, 0)
    for group in range(GROUPS):
        at, span = group * GROUP * PER_OWNER, GROUP * MEMBERS
        far_grad[group * span : (group + 1) * span] = t_dot(
            picks[at : at + LANES], packed[at : at + LANES]
        ).astype(BF16)

    def recv_step(step, carry):
        at = pl.ds(pl.multiple_of(step * LANES, LANES), LANES)
        got = summed(receivers[...], step * LANES, LANES).astype(BF16)
        node_grad[at] += dot_t(got, recv_w[...])
        return carry

    lax.fori_loop(0, NODES // LANES, recv_step, 0)

    for step in range(STEPS):
        at = pl.ds(step * STEP, STEP)
        pltpu.make_async_copy(new_v.at[at], edge_new.at[at], new_sem.at[step]).wait()
        pltpu.make_async_copy(grad_v.at[at], edge_grad.at[at], grad_sem.at[step]).wait()


def layer(count, senders, receivers, ext, coarse, nodes, node_up, edges, edge_up, weights, gains):
    vmem = pl.BlockSpec(memory_space=pltpu.VMEM)
    smem = pl.BlockSpec(memory_space=pltpu.SMEM)
    far = pl.BlockSpec(memory_space=pl.ANY)
    return pl.pallas_call(
        layer_kernel,
        out_shape=(
            jax.ShapeDtypeStruct((NODES, D), BF16),
            jax.ShapeDtypeStruct((SLOTS, D), BF16),
            jax.ShapeDtypeStruct((NODES, D), F32),
            jax.ShapeDtypeStruct((SLOTS, D), F32),
            jax.ShapeDtypeStruct((EXT, D), BF16),
            jax.ShapeDtypeStruct((COARSE, D), BF16),
        ),
        in_specs=[smem, vmem, vmem, vmem, vmem, vmem, vmem, far, far] + [vmem] * 9,
        out_specs=(vmem, far, vmem, far, vmem, vmem),
        scratch_shapes=[
            pltpu.VMEM((SLOTS, D), BF16),
            pltpu.VMEM((SLOTS, D), BF16),
            pltpu.VMEM((SLOTS, D), BF16),
            pltpu.VMEM((SLOTS, D), F32),
            pltpu.VMEM((TABLE, D), BF16),
            pltpu.VMEM((STEP, TABLE), BF16),
            pltpu.VMEM((PACKED, D), BF16),
            pltpu.VMEM((PACKED, GROUP * MEMBERS), BF16),
            pltpu.VMEM((OWNERS, LANES), F32),
            pltpu.VMEM((8, SLOTS), jnp.int32),
            pltpu.VMEM((SLOTS, D), BF16),
            pltpu.VMEM((SLOTS, D), BF16),
            pltpu.VMEM((SLOTS, LANES), F32),
            pltpu.VMEM((SLOTS, D), BF16),
            pltpu.VMEM((NODES, D), F32),
            pltpu.VMEM((NODES, D), BF16),
            pltpu.SemaphoreType.DMA((STEPS,)),
            pltpu.SemaphoreType.DMA((STEPS,)),
            pltpu.SemaphoreType.DMA((STEPS,)),
            pltpu.SemaphoreType.DMA((STEPS,)),
        ],
        compiler_params=pltpu.CompilerParams(vmem_limit_bytes=VMEM_BYTES),
        name="layer",
    )(count, senders, receivers, ext, coarse, nodes, node_up, edges, edge_up, *weights, *gains)


def body(
    node_latents,
    edge_latents,
    senders,
    receivers,
    edge_count,
    edge_self_w,
    edge_send_w,
    edge_recv_w,
    edge_out_w,
    node_self_w,
    node_aggr_w,
    node_out_w,
    edge_gain,
    node_gain,
    node_upstream,
    edge_upstream,
):
    ext, coarse = spread(node_latents)
    weights = (edge_self_w, edge_send_w, edge_recv_w, edge_out_w, node_self_w, node_aggr_w, node_out_w)
    gains = (edge_gain.reshape(1, D), node_gain.reshape(1, D))
    node_new, edge_new, node_grad, edge_grad, rim, far_grad = layer(
        edge_count,
        senders.reshape(1, SLOTS),
        receivers.reshape(1, SLOTS),
        ext.reshape(EXT, D),
        coarse.reshape(COARSE, D),
        node_latents.reshape(NODES, D),
        node_upstream.reshape(NODES, D),
        edge_latents.reshape(SLOTS, D),
        edge_upstream.reshape(SLOTS, D),
        weights,
        gains,
    )
    node_grads = collect(
        rim.reshape(4, 5, BLOCK, D), far_grad.reshape(OWNERS, MEMBERS, D), node_grad, edge_send_w
    )
    grid = node_latents.shape
    return (
        node_new.reshape(grid),
        edge_new.reshape(edge_latents.shape),
        node_grads.reshape(grid),
        edge_grad.reshape(edge_latents.shape),
    )


def solution(mesh):
    tiles = P("lat", "lon", None, None)
    lists = P("lat", "lon", None)
    return jax.shard_map(
        body,
        mesh=mesh,
        in_specs=(tiles, tiles, lists, lists, P("lat", "lon")) + (P(),) * 9 + (tiles, tiles),
        out_specs=(tiles,) * 4,
        check_vma=False,
    )
```

time: 1130 us -> 150 us (0.13)
  the two profiles are of different devices: /device:TPU:0 before, /device:TPU:1 now
where the time goes in v1:
time: 150 us; the launch traced here: 149 us
  Pallas kernels  146 us (97%)
  local copies, waits for them, and re-layouts  2.1 us (1%)
    pallas_call x1, Pallas kernels, layer(): pl.pallas_call(layer_kernel, out_shape=(jax.ShapeDtypeStruct((NODES, D),...  65 us
    pallas_call x1, Pallas kernels, collect(): pl.pallas_call(collect_kernel, out_shape=jax.ShapeDtypeStruct((NODES, D),...  40.4 us
    pallas_call x1, Pallas kernels, spread(): pl.pallas_call(spread_kernel, out_shape=(jax.ShapeDtypeStruct((4, 5, BLOC...  40.4 us

profile of v1, /device:TPU:1, one launch (start us, length us, event | category | flops | bytes accessed | tf_op | source)
XLA Modules:
  0.0 149.2 jit_solution(17890442370660807921)
XLA Ops:
  1.3 40.4 %spread.1 = (bf16[4,5,64,512]{3,2,1,0:T(8,128)(2,1)}, bf16[128,16,512]{2,1,0:T(8,128)(2,1)}) custom-call(bf16[2,3,64,512]{3,2,1,0:T(8,128)(2,1)} %nodes.1), custom_call_target="tpu_custom_call" | custom-call | tf_op jit(solution)/shard_map/spread/pallas_call | solution.py:170
  41.7 65.0 %layer.1 = (bf16[384,512]{1,0:T(8,128)(2,1)}, bf16[3072,512]{1,0:T(8,128)(2,1)}, f32[384,512]{1,0:T(8,128)}, f32[3072,512]{1,0:T(8,128)}, bf16[1280,512]{1,0:T(8,128)(2,1)}, /*index=5*/bf16[2048,512]{1,0:T(8,128)(2,1)}) custom-call(s32[1,1]{1,0:T(1,128)S(6)} %copy.21.count, s32[1,3072]{1,0:T(1,128)} %bitcast.25, s32[1,3072]{1,0:T(1,128)} %bitcast.26, ...), custom_call_target="tpu_custom_call" | custom-call | tf_op jit(solution)/shard_map/layer/pallas_call | solution.py:522
  106.7 40.4 %collect.1 = f32[384,512]{1,0:T(8,128)} custom-call(bf16[4,5,64,512]{3,2,1,0:T(8,128)(2,1)} %bitcast.22, bf16[128,16,512]{2,1,0:T(8,128)(2,1)} %bitcast.19, f32[384,512]{1,0:T(8,128)} %get-tuple-element.18.part, bf16[512,512]{1,0:T(8,128)(2,1)} %send_w.3), custom_call_target="tpu_custom_call" | custom-call | tf_op jit(solution)/shard_map/collect/pallas_call | solution.py:312
  147.1 2.1 %copy.22 = f32[2,3,64,512]{3,2,1,0:T(8,128)} copy(f32[2,3,64,512]{3,2,1,0:T(8,128)} %bitcast.16) | data formatting | bytes 1572864

commit v2 on v0

v2 whole, which is shorter than its diff:
```python
import jax
import jax.numpy as jnp
from jax import lax
from jax.experimental import pallas as pl
from jax.experimental.pallas import tpu as pltpu
from jax.sharding import PartitionSpec as P

MESH = pl.DeviceIdType.MESH
F32 = jnp.float32
BF16 = jnp.bfloat16
EPSILON = 1e-05

D = 512
BLOCK = 64
SLOTS = 3072
NODES = 384
EXT = 1280
OWNERS = 128
MEMBERS = 16
COARSE = OWNERS * MEMBERS
PER_OWNER = 8
PACKED = OWNERS * PER_OWNER
STEP = 256
STEPS = SLOTS // STEP
LANES = 128
GROUP = 16
GROUPS = OWNERS // GROUP
LONS = 32
SAME_CORE = 64
RIM = 14 * BLOCK
VMEM_BYTES = 60 * 1024 * 1024


def dot(left, right):
    return jnp.dot(left, right, preferred_element_type=F32)


def dot_t(left, right):
    return lax.dot_general(left, right, (((1,), (1,)), ((), ())), preferred_element_type=F32)


def t_dot(left, right):
    return lax.dot_general(left, right, (((0,), (0,)), ((), ())), preferred_element_type=F32)


def onehot(mask):
    return jnp.where(mask, 1.0, 0.0).astype(BF16)


def mean(rows):
    return jnp.sum(rows, -1, keepdims=True) * (1.0 / D)


def sigmoid(pre):
    return 0.5 * jnp.tanh(0.5 * pre) + 0.5


def places():
    lat = lax.axis_index("lat")
    lon = lax.axis_index("lon")
    return lat, lon


def shifted(lat, lon, row, col):
    return {"lat": lax.rem(lat + row + 4, 4), "lon": lax.rem(lon + col + LONS, LONS)}


def rings(lat, lon):
    core, x, z = lat % 2, lon // 8, lon // 2 % 4
    y = lat // 2 * 2 + lon % 2
    near = z + core * (x - z)
    far = x + core * (z - x)

    def device(y_step, near_step, far_step):
        y_at = lax.rem(y + y_step, 4)
        x_at = lax.rem(x + far_step + core * (near_step - far_step), 4)
        z_at = lax.rem(z + near_step + core * (far_step - near_step), 4)
        return {"lat": y_at // 2 * 2 + core, "lon": x_at * 8 + z_at * 2 + y_at % 2}

    return core, y, near, far, device


def greet(lat, lon, device):
    peers = [shifted(lat, lon, row, col) for row in (-1, 0, 1) for col in (-1, 0, 1) if row or col]
    for step in (1, 2, 3):
        peers += [device(step, 0, 0), device(0, step, 0), device(0, 0, step)]
    for peer in peers:
        pl.semaphore_signal(pltpu.get_barrier_semaphore(), inc=1, device_id=peer, device_id_type=MESH)
    return len(peers)


def reaches(lat, row):
    return jnp.logical_and(lat + row >= 0, lat + row < 4)


RIM_BASES = (0, 64, 128, 192, 256, 960, 1024, 1088, 1152, 1216, 320, 640, 576, 896)
CORE_BASES = (384, 448, 512, 704, 768, 832)
HALO = (
    ((-1, 0), (0, (0, 3)), (6, 3)),
    ((1, 0), (1, (0, 3)), (1, 3)),
    ((0, -1), (None, 0), (12, 2)),
    ((0, 1), (None, 2), (10, 2)),
    ((-1, -1), (0, (0, 1)), (9, 1)),
    ((-1, 1), (0, (2, 1)), (5, 1)),
    ((1, -1), (1, (0, 1)), (4, 1)),
    ((1, 1), (1, (2, 1)), (0, 1)),
)
BACK = (
    ((-1, 0), (1, 3), (3, 3)),
    ((1, 0), (6, 3), (0, 3)),
    ((0, -1), (10, 2), (8, 2)),
    ((0, 1), (12, 2), (6, 2)),
    ((-1, -1), (0, 1), (13, 1)),
    ((-1, 1), (4, 1), (12, 1)),
    ((1, -1), (5, 1), (11, 1)),
    ((1, 1), (9, 1), (10, 1)),
)


def place_of(owner):
    core = jnp.bitwise_and(jnp.right_shift(owner, 5), 1)
    y = jnp.right_shift(owner, 6) * 2 + jnp.bitwise_and(owner, 1)
    x = jnp.bitwise_and(jnp.right_shift(owner, 3), 3)
    z = jnp.bitwise_and(jnp.right_shift(owner, 1), 3)
    place = jnp.where(core == 0, x * 16 + z * 4, SAME_CORE + z * 16 + x * 4) + y
    return jnp.where(owner < 0, owner, place)


def rows_of(step, size=STEP):
    return pl.ds(pl.multiple_of(step * size, size), size)


def column(ids):
    return jnp.transpose(jnp.broadcast_to(ids, (LANES, STEP)))


def lane_ids(first, second):
    lane = lax.broadcasted_iota(jnp.int32, (STEP, LANES), 1)
    return lane + jnp.where(lane < BLOCK, first, second - BLOCK)


def row_ids(bases):
    row = lax.broadcasted_iota(jnp.int32, (len(bases) * BLOCK, 1), 0)
    block = jnp.right_shift(row, 6)
    start = jnp.zeros_like(row)
    for at, base in enumerate(bases):
        start = jnp.where(block == at, base - at * BLOCK, start)
    return row + start


def rank_slots(senders, slot_of, requests, picks):
    earlier = onehot(
        lax.broadcasted_iota(jnp.int32, (STEP, STEP), 0) < lax.broadcasted_iota(jnp.int32, (STEP, STEP), 1)
    )
    down = lax.broadcasted_iota(jnp.int32, (OWNERS, STEP), 0)
    requests[...] = jnp.zeros_like(requests)

    def rank_step(step, seen):
        at = rows_of(step)
        ids = senders[:, at]
        far = ids - EXT
        owner = place_of(jnp.right_shift(far, 4))
        flags = jnp.where(jnp.broadcast_to(owner, (OWNERS, STEP)) == down, 1.0, 0.0)
        flags_16 = flags.astype(BF16)
        before = dot(flags_16, earlier) + seen
        rank = jnp.sum(flags * before, 0, keepdims=True).astype(jnp.int32)
        slot_of[0:1, at] = jnp.where(far >= 0, EXT + owner * PER_OWNER + rank, ids)
        member = jnp.where(far >= 0, jnp.bitwise_and(far, MEMBERS - 1) + 1, 0).astype(F32)
        chosen = jnp.where(jnp.broadcast_to(rank, (OWNERS, STEP)) == down, jnp.broadcast_to(member, (OWNERS, STEP)), 0.0)
        requests[...] += dot_t(flags_16, chosen.astype(BF16))
        return seen + jnp.sum(flags, 1, keepdims=True)

    lax.fori_loop(0, STEPS, rank_step, jnp.zeros((OWNERS, 1), F32))
    wide = jnp.broadcast_to(requests[...][:, None, :], (OWNERS, PER_OWNER, LANES)).reshape(PACKED, LANES)
    at_row = jnp.bitwise_and(lax.broadcasted_iota(jnp.int32, (PACKED, LANES), 0), PER_OWNER - 1)
    at_lane = lax.broadcasted_iota(jnp.int32, (PACKED, LANES), 1)
    wanted = jnp.sum(jnp.where(at_row == at_lane, wide, 0.0), 1, keepdims=True).astype(jnp.int32)
    span = GROUP * MEMBERS
    rows_in = lax.broadcasted_iota(jnp.int32, (PACKED, span), 0)
    cols_in = lax.broadcasted_iota(jnp.int32, (PACKED, span), 1)
    same = jnp.bitwise_and(jnp.right_shift(rows_in, 3), GROUP - 1) == jnp.right_shift(cols_in, 4)
    named = wanted == jnp.bitwise_and(cols_in, MEMBERS - 1) + 1
    picks[...] = onehot(jnp.logical_and(same, named))


def spread_kernel(
    nodes, senders, receivers, node_rows, edges, self_w, send_w, recv_w,
    pre, slot_of, picks,
    coarse, rim, edges_v, pre_v, weights_v, table, hot, packed, requests,
    load_sem, edges_sem, pre_sem, kept_sem, halo_send, halo_recv,
    y_send, y_recv, near_send, near_recv, far_send, far_recv, pass_send, pass_recv,
):
    lat, lon = places()
    core, y, near, far, device = rings(lat, lon)
    met = greet(lat, lon, device)
    loads = []
    for at, source in enumerate((recv_w, send_w, self_w)):
        copy = pltpu.make_async_copy(source, weights_v.at[at], load_sem.at[at])
        copy.start()
        loads.append(copy)
    for step in range(STEPS):
        at = pl.ds(step * STEP, STEP)
        pltpu.make_async_copy(edges.at[at], edges_v.at[at], edges_sem.at[step]).start()

    base = core * SAME_CORE
    mine = base + far * 16 + near * 4 + y
    first = nodes.at[0, 0, pl.ds(0, MEMBERS)]
    kept = pltpu.make_async_copy(first, coarse.at[mine], kept_sem)
    kept.start()
    rank_slots(senders, slot_of, requests, picks)
    pl.semaphore_wait(pltpu.get_barrier_semaphore(), met)

    def remote(source, target, sems, at, peer):
        return pltpu.make_async_remote_copy(
            src_ref=source,
            dst_ref=target,
            send_sem=sems[0].at[at],
            recv_sem=sems[1].at[at],
            device_id=peer,
            device_id_type=MESH,
        )

    y_copies = [remote(first, coarse.at[mine], (y_send, y_recv), step - 1, device(step, 0, 0)) for step in (1, 2, 3)]
    for copy in y_copies:
        copy.start()
    halos = []
    for at, ((row, col), (r, c), (to, size)) in enumerate(HALO):
        source = nodes.at[pl.ds(0, 2), c] if r is None else nodes.at[r, pl.ds(*c)]
        copy = remote(source, rim.at[pl.ds(to, size)], (halo_send, halo_recv), at, shifted(lat, lon, row, col))
        if row:
            pl.when(reaches(lat, row))(copy.start)
        else:
            copy.start()
        halos.append((row, copy))

    @pl.when(lat == 0)
    def _():
        rim[0:5] = jnp.zeros((5, BLOCK, D), BF16)

    @pl.when(lat == 3)
    def _():
        rim[5:10] = jnp.zeros((5, BLOCK, D), BF16)

    for copy in loads:
        copy.wait()
    table[0:NODES] = dot(node_rows[...], weights_v[0]).astype(BF16)
    table[NODES : 2 * NODES] = dot(node_rows[...], weights_v[1]).astype(BF16)
    core_ids = [lane_ids(CORE_BASES[at], CORE_BASES[at + 1]) for at in (0, 2, 4)]
    own_ids = [lane_ids(at * LANES, at * LANES + BLOCK) for at in range(3)]
    rim_ids = [lane_ids(RIM_BASES[at], RIM_BASES[at + 1]) for at in range(0, 14, 2)]
    far_ids = [lane_ids(EXT + at * LANES, EXT + at * LANES + BLOCK) for at in range(PACKED // LANES)]

    def own_step(step, carry):
        at = rows_of(step)
        from_col = column(slot_of[0:1, at])
        to_col = column(receivers[:, at])
        for group in range(3):
            hot[:, group * LANES : (group + 1) * LANES] = onehot(to_col == own_ids[group])
            hot[:, NODES + group * LANES : NODES + (group + 1) * LANES] = onehot(from_col == core_ids[group])
        pltpu.make_async_copy(edges.at[at], edges_v.at[at], edges_sem.at[step]).wait()
        pre_v[at] = dot(edges_v[at], weights_v[2]) + dot(hot[:, : 2 * NODES], table[: 2 * NODES])
        return carry

    def rim_step(step, carry):
        at = rows_of(step)
        from_col = column(slot_of[0:1, at])
        for group in range(RIM // LANES):
            hot[:, group * LANES : (group + 1) * LANES] = onehot(from_col == rim_ids[group])
        pre_v[at] += dot(hot[:, :RIM], table[:RIM])
        return carry

    def far_step(step, carry):
        at = rows_of(step)
        from_col = column(slot_of[0:1, at])
        for group in range(PACKED // LANES):
            hot[:, group * LANES : (group + 1) * LANES] = onehot(from_col == far_ids[group])
        pre_v[at] += dot(hot[...], table[...])
        pltpu.make_async_copy(pre_v.at[at], pre.at[at], pre_sem.at[step]).start()
        return carry

    lax.fori_loop(0, 4, own_step, 0)
    kept.wait()
    for copy in y_copies:
        copy.wait_recv()

    def piece(step):
        return coarse.at[pl.ds(base + far * 16 + lax.rem(near + 4 - step, 4) * 4, 4)]

    near_copies = [remote(piece(0), piece(0), (near_send, near_recv), step - 1, device(0, step, 0)) for step in (1, 3, 2)]
    for copy in near_copies:
        copy.start()
    far_copies = {}

    def send_far(part):
        for step in (1, 3, 2):
            copy = remote(piece(part), piece(part), (far_send, far_recv), part * 3 + step - 1, device(0, 0, step))
            copy.start()
            far_copies[part, step] = copy

    send_far(0)
    lax.fori_loop(4, 8, own_step, 0)
    for part, copy in zip((1, 3, 2), near_copies):
        copy.wait_recv()
        send_far(part)
    partner = shifted(lat, lon, 1 - 2 * core, 0)
    passes = []

    def hand_over(step):
        block = coarse.at[pl.ds(base + lax.rem(far + 4 - step, 4) * 16, 16)]
        copy = remote(block, block, (pass_send, pass_recv), step, partner)
        copy.start()
        passes.append(copy)

    hand_over(0)
    lax.fori_loop(8, STEPS, own_step, 0)
    for row, copy in halos:
        if row:
            pl.when(reaches(lat, -row))(copy.wait_recv)
        else:
            copy.wait_recv()
    table[:RIM] = dot(rim[...].reshape(RIM, D), weights_v[1]).astype(BF16)
    lax.fori_loop(0, STEPS // 2, rim_step, 0)
    for part in range(4):
        far_copies[part, 1].wait_recv()
    hand_over(1)
    lax.fori_loop(STEPS // 2, STEPS, rim_step, 0)
    for step in (3, 2):
        for part in range(4):
            far_copies[part, step].wait_recv()
        hand_over(step)
    for copy in passes:
        copy.wait_recv()
    for group in range(GROUPS):
        at, span = group * LANES, GROUP
        packed[at : at + LANES] = dot(
            picks[at : at + LANES], coarse[group * span : (group + 1) * span].reshape(GROUP * MEMBERS, D)
        ).astype(BF16)
    table[...] = dot(packed[...], weights_v[1]).astype(BF16)
    lax.fori_loop(0, STEPS, far_step, 0)
    for step in range(STEPS):
        at = pl.ds(step * STEP, STEP)
        pltpu.make_async_copy(pre_v.at[at], pre.at[at], pre_sem.at[step]).wait()
    for row, copy in halos:
        if row:
            pl.when(reaches(lat, row))(copy.wait_send)
        else:
            copy.wait_send()
    for copy in y_copies + near_copies + list(far_copies.values()) + passes:
        copy.wait_send()


def spread(nodes, senders, receivers, node_rows, edges, self_w, send_w, recv_w):
    vmem = pl.BlockSpec(memory_space=pltpu.VMEM)
    hbm = pl.BlockSpec(memory_space=pl.ANY)
    dma = pltpu.SemaphoreType.DMA
    return pl.pallas_call(
        spread_kernel,
        out_shape=(
            jax.ShapeDtypeStruct((SLOTS, D), F32),
            jax.ShapeDtypeStruct((8, SLOTS), jnp.int32),
            jax.ShapeDtypeStruct((PACKED, GROUP * MEMBERS), BF16),
        ),
        in_specs=[hbm, vmem, vmem, vmem, hbm, hbm, hbm, hbm],
        out_specs=(hbm, vmem, vmem),
        scratch_shapes=[
            pltpu.VMEM((OWNERS, MEMBERS, D), BF16),
            pltpu.VMEM((14, BLOCK, D), BF16),
            pltpu.VMEM((SLOTS, D), BF16),
            pltpu.VMEM((SLOTS, D), F32),
            pltpu.VMEM((3, D, D), BF16),
            pltpu.VMEM((PACKED, D), BF16),
            pltpu.VMEM((STEP, PACKED), BF16),
            pltpu.VMEM((PACKED, D), BF16),
            pltpu.VMEM((OWNERS, LANES), F32),
            dma((3,)), dma((STEPS,)), dma((STEPS,)), dma, dma((8,)), dma((8,)),
            dma((3,)), dma((3,)), dma((3,)), dma((3,)), dma((12,)), dma((12,)), dma((4,)), dma((4,)),
        ],
        compiler_params=pltpu.CompilerParams(
            collective_id=0, has_side_effects=True, vmem_limit_bytes=VMEM_BYTES
        ),
        name="spread",
    )(nodes, senders, receivers, node_rows, edges, self_w, send_w, recv_w)


def collect_kernel(
    far_grad, slot_of, receivers, pre_grad, send_w, recv_w, out,
    pre_grad_v, own_far, paired, summed, far_in, near_sum, near_in, y_sum, y_in, rim, rim_in, total,
    load_sem, halo_send, halo_recv, pair_send, pair_recv, far_send, far_recv, near_send, near_recv, y_send, y_recv,
):
    lat, lon = places()
    core, y, near, far, device = rings(lat, lon)
    met = greet(lat, lon, device)
    partner = shifted(lat, lon, 1 - 2 * core, 0)
    load = pltpu.make_async_copy(pre_grad, pre_grad_v, load_sem.at[0])
    load.start()
    load_far = pltpu.make_async_copy(far_grad.at[pl.ds(core * SAME_CORE, SAME_CORE)], own_far, load_sem.at[1])
    load_far.start()

    def remote(source, target, sems, at, peer):
        return pltpu.make_async_remote_copy(
            src_ref=source,
            dst_ref=target,
            send_sem=sems[0].at[at],
            recv_sem=sems[1].at[at],
            device_id=peer,
            device_id_type=MESH,
        )

    @pl.when(lat == 0)
    def _():
        rim_in[0:3] = jnp.zeros((3, BLOCK, D), BF16)
        rim_in[10:12] = jnp.zeros((2, BLOCK, D), BF16)

    @pl.when(lat == 3)
    def _():
        rim_in[3:6] = jnp.zeros((3, BLOCK, D), BF16)
        rim_in[12:14] = jnp.zeros((2, BLOCK, D), BF16)

    pl.semaphore_wait(pltpu.get_barrier_semaphore(), met)
    pairs = []
    for step in (1, 3, 2, 0):
        at = lax.rem(near + step, 4) * 16
        copy = remote(
            far_grad.at[pl.ds((1 - core) * SAME_CORE + at, 16)], paired.at[pl.ds(at, 16)], (pair_send, pair_recv), step, partner
        )
        copy.start()
        pairs.append((step, copy))

    def gathered(ids, bases):
        rows = row_ids(bases)
        mask = jnp.broadcast_to(ids, (rows.shape[0], SLOTS)) == rows
        return dot(onehot(mask), pre_grad_v[...])

    load.wait()
    slots = slot_of[0:1, :]
    rim[0:5] = gathered(slots, RIM_BASES[0:5]).astype(BF16).reshape(5, BLOCK, D)
    rim[5:10] = gathered(slots, RIM_BASES[5:10]).astype(BF16).reshape(5, BLOCK, D)
    rim[10:14] = gathered(slots, RIM_BASES[10:14]).astype(BF16).reshape(4, BLOCK, D)
    halos = []
    for at, ((row, col), (start, size), (to, _)) in enumerate(BACK):
        copy = remote(
            rim.at[pl.ds(start, size)], rim_in.at[pl.ds(to, size)], (halo_send, halo_recv), at, shifted(lat, lon, row, col)
        )
        if row:
            pl.when(reaches(lat, row))(copy.start)
        else:
            copy.start()
        halos.append((row, copy))

    load_far.wait()
    copies = []
    for step, copy in pairs:
        copy.wait_recv()
        at = lax.rem(far + step, 4) * 16
        for row in range(16):
            summed[at + row] = (own_far[at + row].astype(F32) + paired[at + row].astype(F32)).astype(BF16)
        if step:
            sent = remote(
                summed.at[pl.ds(at, 16)], far_in.at[step - 1], (far_send, far_recv), step - 1, device(0, 0, step)
            )
            sent.start()
            copies.append(sent)

    total[...] = gathered(slots, CORE_BASES)
    got = gathered(receivers[...], tuple(range(0, NODES, BLOCK))).astype(BF16)
    out[...] = dot_t(got, recv_w[...])

    for copy in copies:
        copy.wait_recv()
    waiting = list(copies)
    copies = []
    for step in (1, 3, 2, 0):
        at = lax.rem(near + step, 4) * 4
        for row in range(4):
            acc = summed[far * 16 + at + row].astype(F32)
            for peer in range(3):
                acc += far_in[peer, at + row].astype(F32)
            near_sum[at + row] = acc.astype(BF16)
        if step:
            sent = remote(
                near_sum.at[pl.ds(at, 4)], near_in.at[step - 1], (near_send, near_recv), step - 1, device(0, step, 0)
            )
            sent.start()
            copies.append(sent)

    for row, copy in halos:
        if row:
            pl.when(reaches(lat, -row))(copy.wait_recv)
        else:
            copy.wait_recv()

    def add(at, block):
        total[at * BLOCK : (at + 1) * BLOCK] += rim_in[block].astype(F32)

    for block in range(6):
        add(block, block)
    for at, block in ((0, 6), (3, 7), (2, 8), (5, 9), (0, 10), (2, 11), (3, 12), (5, 13)):
        add(at, block)
    out[BLOCK:] += dot_t(total[BLOCK:].astype(BF16), send_w[...])

    for copy in copies:
        copy.wait_recv()
    waiting += copies
    copies = []
    for step in (1, 3, 2, 0):
        at = lax.rem(y + step, 4)
        acc = near_sum[near * 4 + at].astype(F32)
        for peer in range(3):
            acc += near_in[peer, at].astype(F32)
        if step:
            y_sum[at] = acc.astype(BF16)
            sent = remote(y_sum.at[at], y_in.at[step - 1], (y_send, y_recv), step - 1, device(step, 0, 0))
            sent.start()
            copies.append(sent)
    for copy in copies:
        copy.wait_recv()
    waiting += copies
    for peer in range(3):
        acc += y_in[peer].astype(F32)
    total[:MEMBERS] += acc
    out[:BLOCK] += dot_t(total[:BLOCK].astype(BF16), send_w[...])
    for row, copy in halos:
        if row:
            pl.when(reaches(lat, row))(copy.wait_send)
        else:
            copy.wait_send()
    for copy in waiting + [copy for _, copy in pairs]:
        copy.wait_send()


def collect(far_grad, slot_of, receivers, pre_grad, send_w, recv_w):
    vmem = pl.BlockSpec(memory_space=pltpu.VMEM)
    hbm = pl.BlockSpec(memory_space=pl.ANY)
    dma = pltpu.SemaphoreType.DMA
    return pl.pallas_call(
        collect_kernel,
        out_shape=jax.ShapeDtypeStruct((NODES, D), F32),
        in_specs=[hbm, vmem, vmem, hbm, vmem, vmem],
        out_specs=vmem,
        scratch_shapes=[
            pltpu.VMEM((SLOTS, D), BF16),
            pltpu.VMEM((SAME_CORE, MEMBERS, D), BF16),
            pltpu.VMEM((SAME_CORE, MEMBERS, D), BF16),
            pltpu.VMEM((SAME_CORE, MEMBERS, D), BF16),
            pltpu.VMEM((3, 16, MEMBERS, D), BF16),
            pltpu.VMEM((16, MEMBERS, D), BF16),
            pltpu.VMEM((3, 4, MEMBERS, D), BF16),
            pltpu.VMEM((4, MEMBERS, D), BF16),
            pltpu.VMEM((3, MEMBERS, D), BF16),
            pltpu.VMEM((14, BLOCK, D), BF16),
            pltpu.VMEM((14, BLOCK, D), BF16),
            pltpu.VMEM((NODES, D), F32),
            dma((2,)), dma((8,)), dma((8,)), dma((4,)), dma((4,)),
            dma((3,)), dma((3,)), dma((3,)), dma((3,)), dma((3,)), dma((3,)),
        ],
        compiler_params=pltpu.CompilerParams(
            collective_id=1, has_side_effects=True, vmem_limit_bytes=VMEM_BYTES
        ),
        name="collect",
    )(far_grad, slot_of, receivers, pre_grad, send_w, recv_w)


def layer_norm(hidden):
    center = hidden - mean(hidden)
    inv_std = lax.rsqrt(mean(center * center) + EPSILON)
    return center * inv_std, inv_std


def norm_back(grad_out, normed, inv_std):
    return inv_std * (grad_out - mean(grad_out) - normed * mean(grad_out * normed))


def layer_kernel(
    count, slot_of, receivers, picks, nodes, node_up, pre, edges, edge_up,
    out_w, self_w, node_w, aggr_w, node_out, edge_gain, node_gain,
    node_new, edge_new, node_grad, edge_grad, pre_grad, far_grad,
    pre_v, edges_v, up_v, new_v, grad_v, packed, normed_v, slope_v, rstd_v, pre_grad_v, aggr, aggr_grad,
    pre_sem, edges_sem, up_sem, new_sem, grad_sem, pre_grad_sem,
):
    for step in range(STEPS):
        at = pl.ds(step * STEP, STEP)
        pltpu.make_async_copy(pre.at[at], pre_v.at[at], pre_sem.at[step]).start()
        pltpu.make_async_copy(edges.at[at], edges_v.at[at], edges_sem.at[step]).start()
    for step in range(STEPS):
        at = pl.ds(step * STEP, STEP)
        pltpu.make_async_copy(edge_up.at[at], up_v.at[at], up_sem.at[step]).start()

    node_row = lax.broadcasted_iota(jnp.int32, (NODES, STEP), 0)
    slot_row = lax.broadcasted_iota(jnp.int32, (STEP, 1), 0)
    own_ids = [lane_ids(at * LANES, at * LANES + BLOCK) for at in range(3)]
    aggr[...] = jnp.zeros_like(aggr)

    def live_of(step):
        return (slot_row + step * STEP < count[0, 0]).astype(F32)

    def forward(step, carry):
        at = rows_of(step)
        pltpu.make_async_copy(pre.at[at], pre_v.at[at], pre_sem.at[step]).wait()
        pltpu.make_async_copy(edges.at[at], edges_v.at[at], edges_sem.at[step]).wait()
        before = pre_v[at]
        gate = sigmoid(before)
        act = before * gate
        slope_v[at] = (gate + act * (1.0 - gate)).astype(BF16)
        normed, rstd = layer_norm(dot(act.astype(BF16), out_w[...]))
        normed_v[at] = normed.astype(BF16)
        rstd_v[at] = jnp.broadcast_to(rstd, (STEP, LANES))
        message = (live_of(step) * normed * edge_gain[...]).astype(BF16)
        new_v[at] = (edges_v[at].astype(F32) + message.astype(F32)).astype(BF16)
        pltpu.make_async_copy(new_v.at[at], edge_new.at[at], new_sem.at[step]).start()
        to_hot = onehot(jnp.broadcast_to(receivers[:, at], (NODES, STEP)) == node_row)
        aggr[...] += dot(to_hot, message)
        return carry

    lax.fori_loop(0, STEPS, forward, 0, unroll=2)

    node_rows = nodes[...]
    node_pre = dot(node_rows, node_w[...]) + dot(aggr[...].astype(BF16), aggr_w[...])
    gate = sigmoid(node_pre)
    act = node_pre * gate
    slope = gate + act * (1.0 - gate)
    normed, rstd = layer_norm(dot(act.astype(BF16), node_out[...]))
    node_new[...] = (node_rows.astype(F32) + normed * node_gain[...]).astype(BF16)
    up = node_up[...].astype(F32)
    hidden_grad = norm_back(up * node_gain[...], normed, rstd).astype(BF16)
    node_pre_grad = (dot_t(hidden_grad, node_out[...]) * slope).astype(BF16)
    node_grad[...] = up + dot_t(node_pre_grad, node_w[...])
    aggr_grad[...] = dot_t(node_pre_grad, aggr_w[...]).astype(BF16)

    def backward(step, carry):
        at = rows_of(step)
        to_col = column(receivers[:, at])
        to_hot = jnp.concatenate([onehot(to_col == ids) for ids in own_ids], axis=1)
        pltpu.make_async_copy(edge_up.at[at], up_v.at[at], up_sem.at[step]).wait()
        upstream = up_v[at].astype(F32)
        grad = live_of(step) * (upstream + dot(to_hot, aggr_grad[...])) * edge_gain[...]
        normed = normed_v[at].astype(F32)
        hidden_grad = norm_back(grad, normed, rstd_v[at][:, :1]).astype(BF16)
        gone = (dot_t(hidden_grad, out_w[...]) * slope_v[at].astype(F32)).astype(BF16)
        pre_grad_v[at] = gone
        pltpu.make_async_copy(pre_grad_v.at[at], pre_grad.at[at], pre_grad_sem.at[step]).start()
        grad_v[at] = upstream + dot_t(gone, self_w[...])
        pltpu.make_async_copy(grad_v.at[at], edge_grad.at[at], grad_sem.at[step]).start()
        return carry

    lax.fori_loop(0, STEPS, backward, 0, unroll=2)

    def far_step(step, carry):
        base = EXT + step * STEP
        mask = jnp.broadcast_to(slot_of[0:1, :], (STEP, SLOTS)) == lax.broadcasted_iota(jnp.int32, (STEP, SLOTS), 0) + base
        packed[rows_of(step)] = dot(onehot(mask), pre_grad_v[...]).astype(BF16)
        return carry

    lax.fori_loop(0, PACKED // STEP, far_step, 0)
    for group in range(GROUPS):
        at, span = group * LANES, GROUP * MEMBERS
        far_grad[group * span : (group + 1) * span] = t_dot(
            picks[at : at + LANES], packed[at : at + LANES]
        ).astype(BF16)

    for step in range(STEPS):
        at = pl.ds(step * STEP, STEP)
        pltpu.make_async_copy(new_v.at[at], edge_new.at[at], new_sem.at[step]).wait()
        pltpu.make_async_copy(pre_grad_v.at[at], pre_grad.at[at], pre_grad_sem.at[step]).wait()
        pltpu.make_async_copy(grad_v.at[at], edge_grad.at[at], grad_sem.at[step]).wait()


def layer(count, slot_of, receivers, picks, nodes, node_up, pre, edges, edge_up, weights, gains):
    vmem = pl.BlockSpec(memory_space=pltpu.VMEM)
    smem = pl.BlockSpec(memory_space=pltpu.SMEM)
    hbm = pl.BlockSpec(memory_space=pl.ANY)
    dma = pltpu.SemaphoreType.DMA
    return pl.pallas_call(
        layer_kernel,
        out_shape=(
            jax.ShapeDtypeStruct((NODES, D), BF16),
            jax.ShapeDtypeStruct((SLOTS, D), BF16),
            jax.ShapeDtypeStruct((NODES, D), F32),
            jax.ShapeDtypeStruct((SLOTS, D), F32),
            jax.ShapeDtypeStruct((SLOTS, D), BF16),
            jax.ShapeDtypeStruct((COARSE, D), BF16),
        ),
        in_specs=[smem] + [vmem] * 5 + [hbm] * 3 + [vmem] * 7,
        out_specs=(vmem, hbm, vmem, hbm, hbm, vmem),
        scratch_shapes=[
            pltpu.VMEM((SLOTS, D), F32),
            pltpu.VMEM((SLOTS, D), BF16),
            pltpu.VMEM((SLOTS, D), BF16),
            pltpu.VMEM((SLOTS, D), BF16),
            pltpu.VMEM((SLOTS, D), F32),
            pltpu.VMEM((PACKED, D), BF16),
            pltpu.VMEM((SLOTS, D), BF16),
            pltpu.VMEM((SLOTS, D), BF16),
            pltpu.VMEM((SLOTS, LANES), F32),
            pltpu.VMEM((SLOTS, D), BF16),
            pltpu.VMEM((NODES, D), F32),
            pltpu.VMEM((NODES, D), BF16),
        ]
        + [dma((STEPS,))] * 6,
        compiler_params=pltpu.CompilerParams(vmem_limit_bytes=VMEM_BYTES),
        name="layer",
    )(count, slot_of, receivers, picks, nodes, node_up, pre, edges, edge_up, *weights, *gains)


def body(
    node_latents,
    edge_latents,
    senders,
    receivers,
    edge_count,
    edge_self_w,
    edge_send_w,
    edge_recv_w,
    edge_out_w,
    node_self_w,
    node_aggr_w,
    node_out_w,
    edge_gain,
    node_gain,
    node_upstream,
    edge_upstream,
):
    grid = node_latents.shape
    node_rows = node_latents.reshape(NODES, D)
    edges = edge_latents.reshape(SLOTS, D)
    to = receivers.reshape(1, SLOTS)
    pre, slot_of, picks = spread(
        node_latents, senders.reshape(1, SLOTS), to, node_rows, edges, edge_self_w, edge_send_w, edge_recv_w
    )
    node_new, edge_new, node_grad, edge_grad, pre_grad, far_grad = layer(
        edge_count,
        slot_of,
        to,
        picks,
        node_rows,
        node_upstream.reshape(NODES, D),
        pre,
        edges,
        edge_upstream.reshape(SLOTS, D),
        (edge_out_w, edge_self_w, node_self_w, node_aggr_w, node_out_w),
        (edge_gain.reshape(1, D), node_gain.reshape(1, D)),
    )
    returned = collect(far_grad.reshape(OWNERS, MEMBERS, D), slot_of, to, pre_grad, edge_send_w, edge_recv_w)
    return (
        node_new.reshape(grid),
        edge_new.reshape(edge_latents.shape),
        (node_grad + returned).reshape(grid),
        edge_grad.reshape(edge_latents.shape),
    )


def solution(mesh):
    tiles = P("lat", "lon", None, None)
    lists = P("lat", "lon", None)
    return jax.shard_map(
        body,
        mesh=mesh,
        in_specs=(tiles, tiles, lists, lists, P("lat", "lon")) + (P(),) * 9 + (tiles, tiles),
        out_specs=(tiles,) * 4,
        check_vma=False,
    )
```

time: 1130 us -> 113 us (0.10)
  the two profiles are of different devices: /device:TPU:0 before, /device:TPU:1 now
where the time goes in v2:
time: 113 us
  Pallas kernels  110 us (97%)
  other arithmetic  2.15 us (2%)
  between operations  1.32 us (1%)
    pallas_call x1, Pallas kernels, spread(): pl.pallas_call(spread_kernel, out_shape=(jax.ShapeDtypeStruct((SLOTS, D),...  46.5 us
    pallas_call x1, Pallas kernels, layer(): pl.pallas_call(layer_kernel, out_shape=(jax.ShapeDtypeStruct((NODES, D),...  32.9 us
    pallas_call x1, Pallas kernels, collect(): pl.pallas_call(collect_kernel, out_shape=jax.ShapeDtypeStruct((NODES, D),...  30.4 us

profile of v2, /device:TPU:1, one launch (start us, length us, event | category | flops | bytes accessed | tf_op | source)
XLA Modules:
  0.0 113.2 jit_solution(4489465110744695074)
XLA Ops:
  1.3 46.5 %spread.1 = (f32[3072,512]{1,0:T(8,128)}, s32[8,3072]{1,0:T(8,128)}, bf16[1024,256]{1,0:T(8,128)(2,1)}) custom-call(bf16[2,3,64,512]{3,2,1,0:T(8,128)(2,1)} %nodes.1, s32[1,3072]{1,0:T(1,128)} %bitcast.24, s32[1,3072]{1,0:T(1,128)} %bitcast.21, bf16[384,512]{1,0:T(8,128)(2,1)} %bitcast.15, bf16[3072,512]{1,0:T(8,128)(2,1)} %bitcast.13, ...), custom_call_target="tpu_custom_call" | custom-call | tf_op jit(solution)/shard_map/spread/pallas_call | solution.py:356
  47.7 32.9 %layer.1 = (bf16[384,512]{1,0:T(8,128)(2,1)}, bf16[3072,512]{1,0:T(8,128)(2,1)}, f32[384,512]{1,0:T(8,128)}, f32[3072,512]{1,0:T(8,128)}, bf16[3072,512]{1,0:T(8,128)(2,1)}, /*index=5*/bf16[2048,512]{1,0:T(8,128)(2,1)}) custom-call(s32[1,1]{1,0:T(1,128)S(6)} %copy.20.count, s32[8,3072]{1,0:T(8,128)} %get-tuple-element.13.slot_of, s32[1,3072]{1,0:T(1,128)} %bitcast.22, ...), custom_call_target="tpu_custom_call" | custom-call | tf_op jit(solution)/shard_map/layer/pallas_call | solution.py:672
  80.7 0.0 copy-start
  80.7 30.4 %collect.1 = f32[384,512]{1,0:T(8,128)} custom-call(bf16[128,16,512]{2,1,0:T(8,128)(2,1)} %bitcast.18, s32[8,3072]{1,0:T(8,128)} %get-tuple-element.13.slot_of, s32[1,3072]{1,0:T(1,128)} %bitcast.23, bf16[3072,512]{1,0:T(8,128)(2,1)} %get-tuple-element.20.pre_grad, bf16[512,512]{1,0:T(8,128)(2,1)} %send_w.3, bf16[512,512]{1,0:T(8,128)(2,1)} %recv_w.3), custom_call_target="tpu_custom_call" | custom-call | tf_op jit(solution)/shard_map/collect/pallas_call | solution.py:535
  111.1 0.0 copy-done
  111.1 2.2 %add.3 = f32[384,512]{1,0:T(8,128)} add(f32[384,512]{1,0:T(8,128)S(1)} %copy-done, f32[384,512]{1,0:T(8,128)} %collect.1) | non-fusion elementwise | flops 196608 | bytes 2359296 | tf_op jit(solution)/shard_map/add | solution.py:746
Async XLA Ops:
  80.7 30.4 %copy-start = (f32[384,512]{1,0:T(8,128)S(1)}, f32[384,512]{1,0:T(8,128)}, u32[]{:S(2)}) copy-start(f32[384,512]{1,0:T(8,128)} %get-tuple-element.18) | copy-start | bytes 2359300

commit v3 on v2

--- a/solution.py
+++ b/solution.py
@@ -20,8 +20,11 @@
 COARSE = OWNERS * MEMBERS
 PER_OWNER = 8
 PACKED = OWNERS * PER_OWNER
-STEP = 256
+STEP = 512
 STEPS = SLOTS // STEP
+TURN = 2
+TURNS = STEPS // TURN
+WIDE = STEP * TURN
 LANES = 128
 GROUP = 16
 GROUPS = OWNERS // GROUP
@@ -80,10 +83,13 @@
     return core, y, near, far, device
 
 
+PLANE = tuple((near, y) for near in (0, 1, 3, 2) for y in (0, 1, 3, 2) if near or y)
+
+
 def greet(lat, lon, device):
     peers = [shifted(lat, lon, row, col) for row in (-1, 0, 1) for col in (-1, 0, 1) if row or col]
-    for step in (1, 2, 3):
-        peers += [device(step, 0, 0), device(0, step, 0), device(0, 0, step)]
+    peers += [device(y_step, near_step, 0) for near_step, y_step in PLANE]
+    peers += [device(0, 0, step) for step in (1, 2, 3)]
     for peer in peers:
         pl.semaphore_signal(pltpu.get_barrier_semaphore(), inc=1, device_id=peer, device_id_type=MESH)
     return len(peers)
@@ -130,6 +136,18 @@
     return pl.ds(pl.multiple_of(step * size, size), size)
 
 
+def turn_of(turn):
+    return rows_of(turn, WIDE)
+
+
+def steps_of(turn):
+    return [rows_of(turn * TURN + step) for step in range(TURN)]
+
+
+def hot_rows(col, groups):
+    return jnp.concatenate([onehot(col == ids) for ids in groups], axis=1)
+
+
 def column(ids):
     return jnp.transpose(jnp.broadcast_to(ids, (LANES, STEP)))
 
@@ -184,30 +202,33 @@
 
 
 def spread_kernel(
-    nodes, senders, receivers, node_rows, edges, self_w, send_w, recv_w,
-    pre, slot_of, picks,
-    coarse, rim, edges_v, pre_v, weights_v, table, hot, packed, requests,
-    load_sem, edges_sem, pre_sem, kept_sem, halo_send, halo_recv,
-    y_send, y_recv, near_send, near_recv, far_send, far_recv, pass_send, pass_recv,
+    nodes, senders_in, receivers_in, node_rows_in, edges, self_w, send_w, recv_w,
+    pre, slot_out, picks_out, table_out,
+    coarse, rim, edges_v, pre_v, weights_v, table, packed, requests, senders, receivers, node_rows, slot_of, picks,
+    load_sem, out_sem, edges_sem, pre_sem, halo_send, halo_recv,
+    plane_send, plane_recv, far_send, far_recv, pass_send, pass_recv,
 ):
     lat, lon = places()
     core, y, near, far, device = rings(lat, lon)
     met = greet(lat, lon, device)
     loads = []
-    for at, source in enumerate((recv_w, send_w, self_w)):
-        copy = pltpu.make_async_copy(source, weights_v.at[at], load_sem.at[at])
+    sources = (
+        (senders_in, senders), (receivers_in, receivers), (node_rows_in, node_rows),
+        (recv_w, weights_v.at[0]), (send_w, weights_v.at[1]), (self_w, weights_v.at[2]),
+    )
+    for at, (source, target) in enumerate(sources):
+        copy = pltpu.make_async_copy(source, target, load_sem.at[at])
         copy.start()
         loads.append(copy)
-    for step in range(STEPS):
-        at = pl.ds(step * STEP, STEP)
-        pltpu.make_async_copy(edges.at[at], edges_v.at[at], edges_sem.at[step]).start()
+    for turn in range(TURNS):
+        at = turn_of(turn)
+        pltpu.make_async_copy(edges.at[at], edges_v.at[at], edges_sem.at[turn]).start()
 
     base = core * SAME_CORE
     mine = base + far * 16 + near * 4 + y
     first = nodes.at[0, 0, pl.ds(0, MEMBERS)]
-    kept = pltpu.make_async_copy(first, coarse.at[mine], kept_sem)
+    kept = pltpu.make_async_copy(first, coarse.at[mine], load_sem.at[6])
     kept.start()
-    rank_slots(senders, slot_of, requests, picks)
     pl.semaphore_wait(pltpu.get_barrier_semaphore(), met)
 
     def remote(source, target, sems, at, peer):
@@ -220,9 +241,13 @@
             device_id_type=MESH,
         )
 
-    y_copies = [remote(first, coarse.at[mine], (y_send, y_recv), step - 1, device(step, 0, 0)) for step in (1, 2, 3)]
-    for copy in y_copies:
+    plane = {}
+    for near_step, y_step in PLANE:
+        copy = remote(
+            first, coarse.at[mine], (plane_send, plane_recv), near_step * 4 + y_step, device(y_step, near_step, 0)
+        )
         copy.start()
+        plane[near_step, y_step] = copy
     halos = []
     for at, ((row, col), (r, c), (to, size)) in enumerate(HALO):
         source = nodes.at[pl.ds(0, 2), c] if r is None else nodes.at[r, pl.ds(*c)]
@@ -243,114 +268,107 @@
 
     for copy in loads:
         copy.wait()
+    rank_slots(senders, slot_of, requests, picks)
+    outs = [
+        pltpu.make_async_copy(slot_of, slot_out, out_sem.at[0]),
+        pltpu.make_async_copy(picks, picks_out, out_sem.at[1]),
+    ]
+    for copy in outs:
+        copy.start()
     table[0:NODES] = dot(node_rows[...], weights_v[0]).astype(BF16)
     table[NODES : 2 * NODES] = dot(node_rows[...], weights_v[1]).astype(BF16)
     core_ids = [lane_ids(CORE_BASES[at], CORE_BASES[at + 1]) for at in (0, 2, 4)]
     own_ids = [lane_ids(at * LANES, at * LANES + BLOCK) for at in range(3)]
     rim_ids = [lane_ids(RIM_BASES[at], RIM_BASES[at + 1]) for at in range(0, 14, 2)]
-    far_ids = [lane_ids(EXT + at * LANES, EXT + at * LANES + BLOCK) for at in range(PACKED // LANES)]
-
-    def own_step(step, carry):
-        at = rows_of(step)
-        from_col = column(slot_of[0:1, at])
-        to_col = column(receivers[:, at])
-        for group in range(3):
-            hot[:, group * LANES : (group + 1) * LANES] = onehot(to_col == own_ids[group])
-            hot[:, NODES + group * LANES : NODES + (group + 1) * LANES] = onehot(from_col == core_ids[group])
-        pltpu.make_async_copy(edges.at[at], edges_v.at[at], edges_sem.at[step]).wait()
-        pre_v[at] = dot(edges_v[at], weights_v[2]) + dot(hot[:, : 2 * NODES], table[: 2 * NODES])
+
+    def own_turn(turn, carry):
+        whole = turn_of(turn)
+        pltpu.make_async_copy(edges.at[whole], edges_v.at[whole], edges_sem.at[turn]).wait()
+        for at in steps_of(turn):
+            hot = jnp.concatenate(
+                [hot_rows(column(receivers[:, at]), own_ids), hot_rows(column(slot_of[0:1, at]), core_ids)], axis=1
+            )
+            pre_v[at] = dot(edges_v[at], weights_v[2]) + dot(hot, table[: 2 * NODES])
         return carry
 
-    def rim_step(step, carry):
-        at = rows_of(step)
-        from_col = column(slot_of[0:1, at])
-        for group in range(RIM // LANES):
-            hot[:, group * LANES : (group + 1) * LANES] = onehot(from_col == rim_ids[group])
-        pre_v[at] += dot(hot[:, :RIM], table[:RIM])
+    def rim_turn(turn, carry):
+        whole = turn_of(turn)
+        for at in steps_of(turn):
+            pre_v[at] += dot(hot_rows(column(slot_of[0:1, at]), rim_ids), table[:RIM])
+        pltpu.make_async_copy(pre_v.at[whole], pre.at[whole], pre_sem.at[turn]).start()
         return carry
-
-    def far_step(step, carry):
-        at = rows_of(step)
-        from_col = column(slot_of[0:1, at])
-        for group in range(PACKED // LANES):
-            hot[:, group * LANES : (group + 1) * LANES] = onehot(from_col == far_ids[group])
-        pre_v[at] += dot(hot[...], table[...])
-        pltpu.make_async_copy(pre_v.at[at], pre.at[at], pre_sem.at[step]).start()
-        return carry
-
-    lax.fori_loop(0, 4, own_step, 0)
-    kept.wait()
-    for copy in y_copies:
-        copy.wait_recv()
 
     def piece(step):
         return coarse.at[pl.ds(base + far * 16 + lax.rem(near + 4 - step, 4) * 4, 4)]
 
-    near_copies = [remote(piece(0), piece(0), (near_send, near_recv), step - 1, device(0, step, 0)) for step in (1, 3, 2)]
-    for copy in near_copies:
-        copy.start()
     far_copies = {}
 
     def send_far(part):
+        for y_step in range(4):
+            if (part, y_step) in plane:
+                plane[part, y_step].wait_recv()
         for step in (1, 3, 2):
             copy = remote(piece(part), piece(part), (far_send, far_recv), part * 3 + step - 1, device(0, 0, step))
             copy.start()
             far_copies[part, step] = copy
 
-    send_far(0)
-    lax.fori_loop(4, 8, own_step, 0)
-    for part, copy in zip((1, 3, 2), near_copies):
-        copy.wait_recv()
-        send_far(part)
     partner = shifted(lat, lon, 1 - 2 * core, 0)
     passes = []
 
     def hand_over(step):
+        if step:
+            for part in range(4):
+                far_copies[part, step].wait_recv()
         block = coarse.at[pl.ds(base + lax.rem(far + 4 - step, 4) * 16, 16)]
         copy = remote(block, block, (pass_send, pass_recv), step, partner)
         copy.start()
         passes.append(copy)
 
+    def pack(group):
+        at = pl.ds(pl.multiple_of(group * LANES, LANES), LANES)
+        rows = dot(picks[at], coarse[pl.ds(group * GROUP, GROUP)].reshape(GROUP * MEMBERS, D)).astype(BF16)
+        packed[at] = dot(rows, weights_v[1]).astype(BF16)
+
+    kept.wait()
+    send_far(0)
+    for part in (1, 3, 2):
+        send_far(part)
     hand_over(0)
-    lax.fori_loop(8, STEPS, own_step, 0)
+    lax.fori_loop(0, TURNS, own_turn, 0)
     for row, copy in halos:
         if row:
             pl.when(reaches(lat, -row))(copy.wait_recv)
         else:
             copy.wait_recv()
-    table[:RIM] = dot(rim[...].reshape(RIM, D), weights_v[1]).astype(BF16)
-    lax.fori_loop(0, STEPS // 2, rim_step, 0)
-    for part in range(4):
-        far_copies[part, 1].wait_recv()
+    table[...] = dot(rim[...].reshape(RIM, D), weights_v[1]).astype(BF16)
+    lax.fori_loop(0, 1, rim_turn, 0)
     hand_over(1)
-    lax.fori_loop(STEPS // 2, STEPS, rim_step, 0)
+    lax.fori_loop(1, TURNS, rim_turn, 0)
     for step in (3, 2):
-        for part in range(4):
-            far_copies[part, step].wait_recv()
         hand_over(step)
+    for step in range(4):
+        pack(core * 4 + step)
     for copy in passes:
         copy.wait_recv()
-    for group in range(GROUPS):
-        at, span = group * LANES, GROUP
-        packed[at : at + LANES] = dot(
-            picks[at : at + LANES], coarse[group * span : (group + 1) * span].reshape(GROUP * MEMBERS, D)
-        ).astype(BF16)
-    table[...] = dot(packed[...], weights_v[1]).astype(BF16)
-    lax.fori_loop(0, STEPS, far_step, 0)
-    for step in range(STEPS):
-        at = pl.ds(step * STEP, STEP)
-        pltpu.make_async_copy(pre_v.at[at], pre.at[at], pre_sem.at[step]).wait()
+    for step in range(4):
+        pack(4 - core * 4 + step)
+    copy = pltpu.make_async_copy(packed, table_out, out_sem.at[2])
+    copy.start()
+    for turn in range(TURNS):
+        at = turn_of(turn)
+        pltpu.make_async_copy(pre_v.at[at], pre.at[at], pre_sem.at[turn]).wait()
+    for copy in outs + [copy]:
+        copy.wait()
     for row, copy in halos:
         if row:
             pl.when(reaches(lat, row))(copy.wait_send)
         else:
             copy.wait_send()
-    for copy in y_copies + near_copies + list(far_copies.values()) + passes:
+    for copy in list(plane.values()) + list(far_copies.values()) + passes:
         copy.wait_send()
 
 
 def spread(nodes, senders, receivers, node_rows, edges, self_w, send_w, recv_w):
-    vmem = pl.BlockSpec(memory_space=pltpu.VMEM)
     hbm = pl.BlockSpec(memory_space=pl.ANY)
     dma = pltpu.SemaphoreType.DMA
     return pl.pallas_call(
@@ -359,21 +377,26 @@
             jax.ShapeDtypeStruct((SLOTS, D), F32),
             jax.ShapeDtypeStruct((8, SLOTS), jnp.int32),
             jax.ShapeDtypeStruct((PACKED, GROUP * MEMBERS), BF16),
+            jax.ShapeDtypeStruct((PACKED, D), BF16),
         ),
-        in_specs=[hbm, vmem, vmem, vmem, hbm, hbm, hbm, hbm],
-        out_specs=(hbm, vmem, vmem),
+        in_specs=[hbm] * 8,
+        out_specs=(hbm,) * 4,
         scratch_shapes=[
             pltpu.VMEM((OWNERS, MEMBERS, D), BF16),
             pltpu.VMEM((14, BLOCK, D), BF16),
             pltpu.VMEM((SLOTS, D), BF16),
             pltpu.VMEM((SLOTS, D), F32),
             pltpu.VMEM((3, D, D), BF16),
-            pltpu.VMEM((PACKED, D), BF16),
-            pltpu.VMEM((STEP, PACKED), BF16),
+            pltpu.VMEM((RIM, D), BF16),
             pltpu.VMEM((PACKED, D), BF16),
             pltpu.VMEM((OWNERS, LANES), F32),
-            dma((3,)), dma((STEPS,)), dma((STEPS,)), dma, dma((8,)), dma((8,)),
-            dma((3,)), dma((3,)), dma((3,)), dma((3,)), dma((12,)), dma((12,)), dma((4,)), dma((4,)),
+            pltpu.VMEM((1, SLOTS), jnp.int32),
+            pltpu.VMEM((1, SLOTS), jnp.int32),
+            pltpu.VMEM((NODES, D), BF16),
+            pltpu.VMEM((8, SLOTS), jnp.int32),
+            pltpu.VMEM((PACKED, GROUP * MEMBERS), BF16),
+            dma((7,)), dma((3,)), dma((TURNS,)), dma((TURNS,)), dma((8,)), dma((8,)),
+            dma((16,)), dma((16,)), dma((12,)), dma((12,)), dma((4,)), dma((4,)),
         ],
         compiler_params=pltpu.CompilerParams(
             collective_id=0, has_side_effects=True, vmem_limit_bytes=VMEM_BYTES
@@ -383,18 +406,24 @@
 
 
 def collect_kernel(
-    far_grad, slot_of, receivers, pre_grad, send_w, recv_w, out,
-    pre_grad_v, own_far, paired, summed, far_in, near_sum, near_in, y_sum, y_in, rim, rim_in, total,
-    load_sem, halo_send, halo_recv, pair_send, pair_recv, far_send, far_recv, near_send, near_recv, y_send, y_recv,
+    far_grad, slot_in, receivers_in, pre_grad, send_in, recv_in, out,
+    pre_grad_v, own_far, paired, summed, far_in, plane_sum, plane_in, rim, rim_in, total,
+    slot_of, receivers, send_w, recv_w,
+    load_sem, halo_send, halo_recv, pair_send, pair_recv, far_send, far_recv, plane_send, plane_recv,
 ):
     lat, lon = places()
     core, y, near, far, device = rings(lat, lon)
     met = greet(lat, lon, device)
     partner = shifted(lat, lon, 1 - 2 * core, 0)
-    load = pltpu.make_async_copy(pre_grad, pre_grad_v, load_sem.at[0])
-    load.start()
-    load_far = pltpu.make_async_copy(far_grad.at[pl.ds(core * SAME_CORE, SAME_CORE)], own_far, load_sem.at[1])
-    load_far.start()
+    loads = []
+    sources = (
+        (slot_in, slot_of), (pre_grad, pre_grad_v), (far_grad.at[pl.ds(core * SAME_CORE, SAME_CORE)], own_far),
+        (receivers_in, receivers), (recv_in, recv_w), (send_in, send_w),
+    )
+    for at, (source, target) in enumerate(sources):
+        copy = pltpu.make_async_copy(source, target, load_sem.at[at])
+        copy.start()
+        loads.append(copy)
 
     def remote(source, target, sems, at, peer):
         return pltpu.make_async_remote_copy(
@@ -431,7 +460,8 @@
         mask = jnp.broadcast_to(ids, (rows.shape[0], SLOTS)) == rows
         return dot(onehot(mask), pre_grad_v[...])
 
-    load.wait()
+    for copy in loads:
+        copy.wait()
     slots = slot_of[0:1, :]
     rim[0:5] = gathered(slots, RIM_BASES[0:5]).astype(BF16).reshape(5, BLOCK, D)
     rim[5:10] = gathered(slots, RIM_BASES[5:10]).astype(BF16).reshape(5, BLOCK, D)
@@ -447,7 +477,6 @@
             copy.start()
         halos.append((row, copy))
 
-    load_far.wait()
     copies = []
     for step, copy in pairs:
         copy.wait_recv()
@@ -467,21 +496,20 @@
 
     for copy in copies:
         copy.wait_recv()
-    waiting = list(copies)
-    copies = []
-    for step in (1, 3, 2, 0):
-        at = lax.rem(near + step, 4) * 4
-        for row in range(4):
-            acc = summed[far * 16 + at + row].astype(F32)
-            for peer in range(3):
-                acc += far_in[peer, at + row].astype(F32)
-            near_sum[at + row] = acc.astype(BF16)
-        if step:
+    plane = []
+    for near_step, y_step in PLANE + ((0, 0),):
+        at = lax.rem(near + near_step, 4) * 4 + lax.rem(y + y_step, 4)
+        acc = summed[far * 16 + at].astype(F32)
+        for peer in range(3):
+            acc += far_in[peer, at].astype(F32)
+        if near_step or y_step:
+            plane_sum[at] = acc.astype(BF16)
+            slot = near_step * 4 + y_step - 1
             sent = remote(
-                near_sum.at[pl.ds(at, 4)], near_in.at[step - 1], (near_send, near_recv), step - 1, device(0, step, 0)
+                plane_sum.at[at], plane_in.at[slot], (plane_send, plane_recv), slot, device(y_step, near_step, 0)
             )
             sent.start()
-            copies.append(sent)
+            plane.append(sent)
 
     for row, copy in halos:
         if row:
@@ -498,25 +526,10 @@
         add(at, block)
     out[BLOCK:] += dot_t(total[BLOCK:].astype(BF16), send_w[...])
 
-    for copy in copies:
+    for copy in plane:
         copy.wait_recv()
-    waiting += copies
-    copies = []
-    for step in (1, 3, 2, 0):
-        at = lax.rem(y + step, 4)
-        acc = near_sum[near * 4 + at].astype(F32)
-        for peer in range(3):
-            acc += near_in[peer, at].astype(F32)
-        if step:
-            y_sum[at] = acc.astype(BF16)
-            sent = remote(y_sum.at[at], y_in.at[step - 1], (y_send, y_recv), step - 1, device(step, 0, 0))
-            sent.start()
-            copies.append(sent)
-    for copy in copies:
-        copy.wait_recv()
-    waiting += copies
-    for peer in range(3):
-        acc += y_in[peer].astype(F32)
+    for slot in range(15):
+        acc += plane_in[slot].astype(F32)
     total[:MEMBERS] += acc
     out[:BLOCK] += dot_t(total[:BLOCK].astype(BF16), send_w[...])
     for row, copy in halos:
@@ -524,7 +537,7 @@
             pl.when(reaches(lat, row))(copy.wait_send)
         else:
             copy.wait_send()
-    for copy in waiting + [copy for _, copy in pairs]:
+    for copy in copies + plane + [copy for _, copy in pairs]:
         copy.wait_send()
 
 
@@ -535,7 +548,7 @@
     return pl.pallas_call(
         collect_kernel,
         out_shape=jax.ShapeDtypeStruct((NODES, D), F32),
-        in_specs=[hbm, vmem, vmem, hbm, vmem, vmem],
+        in_specs=[hbm] * 6,
         out_specs=vmem,
         scratch_shapes=[
             pltpu.VMEM((SLOTS, D), BF16),
@@ -544,14 +557,16 @@
             pltpu.VMEM((SAME_CORE, MEMBERS, D), BF16),
             pltpu.VMEM((3, 16, MEMBERS, D), BF16),
             pltpu.VMEM((16, MEMBERS, D), BF16),
-            pltpu.VMEM((3, 4, MEMBERS, D), BF16),
-            pltpu.VMEM((4, MEMBERS, D), BF16),
-            pltpu.VMEM((3, MEMBERS, D), BF16),
+            pltpu.VMEM((15, MEMBERS, D), BF16),
             pltpu.VMEM((14, BLOCK, D), BF16),
             pltpu.VMEM((14, BLOCK, D), BF16),
             pltpu.VMEM((NODES, D), F32),
-            dma((2,)), dma((8,)), dma((8,)), dma((4,)), dma((4,)),
-            dma((3,)), dma((3,)), dma((3,)), dma((3,)), dma((3,)), dma((3,)),
+            pltpu.VMEM((8, SLOTS), jnp.int32),
+            pltpu.VMEM((1, SLOTS), jnp.int32),
+            pltpu.VMEM((D, D), BF16),
+            pltpu.VMEM((D, D), BF16),
+            dma((6,)), dma((8,)), dma((8,)), dma((4,)), dma((4,)),
+            dma((3,)), dma((3,)), dma((15,)), dma((15,)),
         ],
         compiler_params=pltpu.CompilerParams(
             collective_id=1, has_side_effects=True, vmem_limit_bytes=VMEM_BYTES
@@ -560,6 +575,11 @@
     )(far_grad, slot_of, receivers, pre_grad, send_w, recv_w)
 
 
+def centered(weight):
+    rows = weight[...].astype(F32)
+    return (rows - mean(rows)).astype(BF16)
+
+
 def layer_norm(hidden):
     center = hidden - mean(hidden)
     inv_std = lax.rsqrt(mean(center * center) + EPSILON)
@@ -571,47 +591,73 @@
 
 
 def layer_kernel(
-    count, slot_of, receivers, picks, nodes, node_up, pre, edges, edge_up,
+    count, slot_of, receivers, picks, table, nodes, node_up, pre, edges, edge_up,
     out_w, self_w, node_w, aggr_w, node_out, edge_gain, node_gain,
     node_new, edge_new, node_grad, edge_grad, pre_grad, far_grad,
-    pre_v, edges_v, up_v, new_v, grad_v, packed, normed_v, slope_v, rstd_v, pre_grad_v, aggr, aggr_grad,
+    pre_v, edges_v, up_v, new_v, grad_v, packed, normed_v, slope_v, rstd_v, pre_grad_v, aggr, aggr_grad, out_c,
     pre_sem, edges_sem, up_sem, new_sem, grad_sem, pre_grad_sem,
 ):
-    for step in range(STEPS):
-        at = pl.ds(step * STEP, STEP)
-        pltpu.make_async_copy(pre.at[at], pre_v.at[at], pre_sem.at[step]).start()
-        pltpu.make_async_copy(edges.at[at], edges_v.at[at], edges_sem.at[step]).start()
-    for step in range(STEPS):
-        at = pl.ds(step * STEP, STEP)
-        pltpu.make_async_copy(edge_up.at[at], up_v.at[at], up_sem.at[step]).start()
-
-    node_row = lax.broadcasted_iota(jnp.int32, (NODES, STEP), 0)
+    def loaded(turn):
+        at = turn_of(turn)
+        return (
+            pltpu.make_async_copy(pre.at[at], pre_v.at[at], pre_sem.at[turn]),
+            pltpu.make_async_copy(edges.at[at], edges_v.at[at], edges_sem.at[turn]),
+        )
+
+    def raised(turn):
+        at = turn_of(turn)
+        return pltpu.make_async_copy(edge_up.at[at], up_v.at[at], up_sem.at[turn])
+
+    for turn in range(TURNS):
+        for copy in loaded(turn):
+            copy.start()
+    for turn in range(TURNS):
+        raised(turn).start()
+
+    out_c[...] = centered(out_w)
+    node_row = lax.broadcasted_iota(jnp.int32, (NODES, WIDE), 0)
     slot_row = lax.broadcasted_iota(jnp.int32, (STEP, 1), 0)
     own_ids = [lane_ids(at * LANES, at * LANES + BLOCK) for at in range(3)]
+    far_ids = [lane_ids(EXT + at * LANES, EXT + at * LANES + BLOCK) for at in range(PACKED // LANES)]
     aggr[...] = jnp.zeros_like(aggr)
 
     def live_of(step):
         return (slot_row + step * STEP < count[0, 0]).astype(F32)
 
-    def forward(step, carry):
-        at = rows_of(step)
-        pltpu.make_async_copy(pre.at[at], pre_v.at[at], pre_sem.at[step]).wait()
-        pltpu.make_async_copy(edges.at[at], edges_v.at[at], edges_sem.at[step]).wait()
-        before = pre_v[at]
-        gate = sigmoid(before)
-        act = before * gate
-        slope_v[at] = (gate + act * (1.0 - gate)).astype(BF16)
-        normed, rstd = layer_norm(dot(act.astype(BF16), out_w[...]))
-        normed_v[at] = normed.astype(BF16)
-        rstd_v[at] = jnp.broadcast_to(rstd, (STEP, LANES))
-        message = (live_of(step) * normed * edge_gain[...]).astype(BF16)
-        new_v[at] = (edges_v[at].astype(F32) + message.astype(F32)).astype(BF16)
-        pltpu.make_async_copy(new_v.at[at], edge_new.at[at], new_sem.at[step]).start()
-        to_hot = onehot(jnp.broadcast_to(receivers[:, at], (NODES, STEP)) == node_row)
-        aggr[...] += dot(to_hot, message)
+    def stored(turn):
+        at = turn_of(turn)
+        return pltpu.make_async_copy(new_v.at[at], edge_new.at[at], new_sem.at[turn])
+
+    def returned(turn):
+        at = turn_of(turn)
+        return (
+            pltpu.make_async_copy(pre_grad_v.at[at], pre_grad.at[at], pre_grad_sem.at[turn]),
+            pltpu.make_async_copy(grad_v.at[at], edge_grad.at[at], grad_sem.at[turn]),
+        )
+
+    def forward(turn, carry):
+        for copy in loaded(turn):
+            copy.wait()
+        messages = []
+        for step, at in enumerate(steps_of(turn)):
+            before = pre_v[at] + dot(hot_rows(column(slot_of[0:1, at]), far_ids), table[...])
+            gate = sigmoid(before)
+            act = before * gate
+            slope_v[at] = (gate + act * (1.0 - gate)).astype(BF16)
+            center = dot(act.astype(BF16), out_c[...])
+            rstd = live_of(turn * TURN + step) * lax.rsqrt(mean(center * center) + EPSILON)
+            normed = center * rstd
+            normed_v[at] = normed.astype(BF16)
+            rstd_v[at] = jnp.broadcast_to(rstd, (STEP, LANES))
+            message = (normed * edge_gain[...]).astype(BF16)
+            new_v[at] = edges_v[at] + message
+            messages.append(message)
+        to_hot = onehot(jnp.broadcast_to(receivers[:, turn_of(turn)], (NODES, WIDE)) == node_row)
+        aggr[...] += dot(to_hot, jnp.concatenate(messages, axis=0))
+        stored(turn).start()
         return carry
 
-    lax.fori_loop(0, STEPS, forward, 0, unroll=2)
+    lax.fori_loop(0, TURNS, forward, 0)
 
     node_rows = nodes[...]
     node_pre = dot(node_rows, node_w[...]) + dot(aggr[...].astype(BF16), aggr_w[...])
@@ -626,23 +672,22 @@
     node_grad[...] = up + dot_t(node_pre_grad, node_w[...])
     aggr_grad[...] = dot_t(node_pre_grad, aggr_w[...]).astype(BF16)
 
-    def backward(step, carry):
-        at = rows_of(step)
-        to_col = column(receivers[:, at])
-        to_hot = jnp.concatenate([onehot(to_col == ids) for ids in own_ids], axis=1)
-        pltpu.make_async_copy(edge_up.at[at], up_v.at[at], up_sem.at[step]).wait()
-        upstream = up_v[at].astype(F32)
-        grad = live_of(step) * (upstream + dot(to_hot, aggr_grad[...])) * edge_gain[...]
-        normed = normed_v[at].astype(F32)
-        hidden_grad = norm_back(grad, normed, rstd_v[at][:, :1]).astype(BF16)
-        gone = (dot_t(hidden_grad, out_w[...]) * slope_v[at].astype(F32)).astype(BF16)
-        pre_grad_v[at] = gone
-        pltpu.make_async_copy(pre_grad_v.at[at], pre_grad.at[at], pre_grad_sem.at[step]).start()
-        grad_v[at] = upstream + dot_t(gone, self_w[...])
-        pltpu.make_async_copy(grad_v.at[at], edge_grad.at[at], grad_sem.at[step]).start()
+    def backward(turn, carry):
+        raised(turn).wait()
+        for step, at in enumerate(steps_of(turn)):
+            upstream = up_v[at].astype(F32)
+            to_hot = hot_rows(column(receivers[:, at]), own_ids)
+            grad = (upstream + dot(to_hot, aggr_grad[...])) * edge_gain[...]
+            normed = normed_v[at].astype(F32)
+            hidden_grad = (rstd_v[at][:, :1] * (grad - normed * mean(grad * normed))).astype(BF16)
+            gone = dot_t(hidden_grad, out_c[...]).astype(BF16) * slope_v[at]
+            pre_grad_v[at] = gone
+            grad_v[at] = upstream + dot_t(gone, self_w[...])
+        for copy in returned(turn):
+            copy.start()
         return carry
 
-    lax.fori_loop(0, STEPS, backward, 0, unroll=2)
+    lax.fori_loop(0, TURNS, backward, 0)
 
     def far_step(step, carry):
         base = EXT + step * STEP
@@ -657,14 +702,13 @@
             picks[at : at + LANES], packed[at : at + LANES]
         ).astype(BF16)
 
-    for step in range(STEPS):
-        at = pl.ds(step * STEP, STEP)
-        pltpu.make_async_copy(new_v.at[at], edge_new.at[at], new_sem.at[step]).wait()
-        pltpu.make_async_copy(pre_grad_v.at[at], pre_grad.at[at], pre_grad_sem.at[step]).wait()
-        pltpu.make_async_copy(grad_v.at[at], edge_grad.at[at], grad_sem.at[step]).wait()
-
-
-def layer(count, slot_of, receivers, picks, nodes, node_up, pre, edges, edge_up, weights, gains):
+    for turn in range(TURNS):
+        stored(turn).wait()
+        for copy in returned(turn):
+            copy.wait()
+
+
+def layer(count, slot_of, receivers, picks, table, nodes, node_up, pre, edges, edge_up, weights, gains):
     vmem = pl.BlockSpec(memory_space=pltpu.VMEM)
     smem = pl.BlockSpec(memory_space=pltpu.SMEM)
     hbm = pl.BlockSpec(memory_space=pl.ANY)
@@ -679,7 +723,7 @@
             jax.ShapeDtypeStruct((SLOTS, D), BF16),
             jax.ShapeDtypeStruct((COARSE, D), BF16),
         ),
-        in_specs=[smem] + [vmem] * 5 + [hbm] * 3 + [vmem] * 7,
+        in_specs=[smem] + [vmem] * 6 + [hbm] * 3 + [vmem] * 7,
         out_specs=(vmem, hbm, vmem, hbm, hbm, vmem),
         scratch_shapes=[
             pltpu.VMEM((SLOTS, D), F32),
@@ -694,11 +738,12 @@
             pltpu.VMEM((SLOTS, D), BF16),
             pltpu.VMEM((NODES, D), F32),
             pltpu.VMEM((NODES, D), BF16),
+            pltpu.VMEM((D, D), BF16),
         ]
-        + [dma((STEPS,))] * 6,
+        + [dma((TURNS,))] * 6,
         compiler_params=pltpu.CompilerParams(vmem_limit_bytes=VMEM_BYTES),
         name="layer",
-    )(count, slot_of, receivers, picks, nodes, node_up, pre, edges, edge_up, *weights, *gains)
+    )(count, slot_of, receivers, picks, table, nodes, node_up, pre, edges, edge_up, *weights, *gains)
 
 
 def body(
@@ -723,7 +768,7 @@
     node_rows = node_latents.reshape(NODES, D)
     edges = edge_latents.reshape(SLOTS, D)
     to = receivers.reshape(1, SLOTS)
-    pre, slot_of, picks = spread(
+    pre, slot_of, picks, table = spread(
         node_latents, senders.reshape(1, SLOTS), to, node_rows, edges, edge_self_w, edge_send_w, edge_recv_w
     )
     node_new, edge_new, node_grad, edge_grad, pre_grad, far_grad = layer(
@@ -731,6 +776,7 @@
         slot_of,
         to,
         picks,
+        table,
         node_rows,
         node_upstream.reshape(NODES, D),
         pre,

time: 113 us -> 95.6 us (0.85)
  Pallas kernels: 110 us -> 92 us
    pallas_call x1, Pallas kernels: 46.5 us -> 34.9 us  [spread(): pl.pallas_call(spread_kernel, out_shape=(jax.ShapeDtypeStruct((SLOTS, D),...]
    pallas_call x1, Pallas kernels: 32.9 us -> 27.8 us  [layer(): pl.pallas_call(layer_kernel, out_shape=(jax.ShapeDtypeStruct((NODES, D),...]
    pallas_call x1, Pallas kernels: 30.4 us -> 29.2 us  [collect(): pl.pallas_call(collect_kernel, out_shape=jax.ShapeDtypeStruct((NODES, D),...]
where the time goes in v3:
time: 95.6 us; the launch traced here: 95.5 us
  Pallas kernels  92 us (96%)
  other arithmetic  2.15 us (2%)
  between operations  1.32 us (1%)
    pallas_call x1, Pallas kernels, spread(): pl.pallas_call(spread_kernel, out_shape=(jax.ShapeDtypeStruct((SLOTS, D),...  34.9 us
    pallas_call x1, Pallas kernels, collect(): pl.pallas_call(collect_kernel, out_shape=jax.ShapeDtypeStruct((NODES, D),...  29.2 us
    pallas_call x1, Pallas kernels, layer(): pl.pallas_call(layer_kernel, out_shape=(jax.ShapeDtypeStruct((NODES, D),...  27.8 us
    add x1, other arithmetic, body(): node_grad + returned  2.15 us

profile of v3, /device:TPU:1, one launch (start us, length us, event | category | flops | bytes accessed | tf_op | source)
XLA Modules:
  0.0 95.5 jit_solution(5391799711803990814)
XLA Ops:
  1.3 34.9 %spread.1 = (f32[3072,512]{1,0:T(8,128)}, s32[8,3072]{1,0:T(8,128)}, bf16[1024,256]{1,0:T(8,128)(2,1)}, bf16[1024,512]{1,0:T(8,128)(2,1)}) custom-call(bf16[2,3,64,512]{3,2,1,0:T(8,128)(2,1)} %nodes.1, s32[1,3072]{1,0:T(1,128)} %bitcast.24, s32[1,3072]{1,0:T(1,128)} %bitcast.21, bf16[384,512]{1,0:T(8,128)(2,1)} %bitcast.15, bf16[3072,512]{1,0:T(8,128)(2,1)} %bitcast.13, ...), custom_call_target="tpu_custom_call" | custom-call | tf_op jit(solution)/shard_map/spread/pallas_call | solution.py:374
  36.2 27.8 %layer.1 = (bf16[384,512]{1,0:T(8,128)(2,1)}, bf16[3072,512]{1,0:T(8,128)(2,1)}, f32[384,512]{1,0:T(8,128)}, f32[3072,512]{1,0:T(8,128)}, bf16[3072,512]{1,0:T(8,128)(2,1)}, /*index=5*/bf16[2048,512]{1,0:T(8,128)(2,1)}) custom-call(s32[1,1]{1,0:T(1,128)S(6)} %copy.20.count, s32[8,3072]{1,0:T(8,128)} %get-tuple-element.14.slot_of.slot_in, ...), custom_call_target="tpu_custom_call" | custom-call | tf_op jit(solution)/shard_map/layer/pallas_call | solution.py:716
  64.0 0.0 copy-start
  64.1 29.2 %collect.1 = f32[384,512]{1,0:T(8,128)} custom-call(bf16[128,16,512]{2,1,0:T(8,128)(2,1)} %bitcast.18, s32[8,3072]{1,0:T(8,128)} %get-tuple-element.14.slot_of.slot_in, s32[1,3072]{1,0:T(1,128)} %bitcast.23, bf16[3072,512]{1,0:T(8,128)(2,1)} %get-tuple-element.22.pre_grad, bf16[512,512]{1,0:T(8,128)(2,1)} %send_in.1, bf16[512,512]{1,0:T(8,128)(2,1)} %recv_in.1), custom_call_target="tpu_custom_call" | custom-call | tf_op jit(solution)/shard_map/collect/pallas_call | solution.py:548
  93.3 0.0 copy-done
  93.3 2.2 %add.3 = f32[384,512]{1,0:T(8,128)} add(f32[384,512]{1,0:T(8,128)S(1)} %copy-done, f32[384,512]{1,0:T(8,128)} %collect.1) | non-fusion elementwise | flops 196608 | bytes 2359296 | tf_op jit(solution)/shard_map/add | solution.py:792
Async XLA Ops:
  64.0 29.2 %copy-start = (f32[384,512]{1,0:T(8,128)S(1)}, f32[384,512]{1,0:T(8,128)}, u32[]{:S(2)}) copy-start(f32[384,512]{1,0:T(8,128)} %get-tuple-element.20) | copy-start | bytes 2359300

commit v4 on v3

--- a/solution.py
+++ b/solution.py
@@ -204,7 +204,7 @@
 def spread_kernel(
     nodes, senders_in, receivers_in, node_rows_in, edges, self_w, send_w, recv_w,
     pre, slot_out, picks_out, table_out,
-    coarse, rim, edges_v, pre_v, weights_v, table, packed, requests, senders, receivers, node_rows, slot_of, picks,
+    coarse, rim, edges_v, pre_v, pre_out, weights_v, table, packed, requests, senders, receivers, node_rows, slot_of, picks,
     load_sem, out_sem, edges_sem, pre_sem, halo_send, halo_recv,
     plane_send, plane_recv, far_send, far_recv, pass_send, pass_recv,
 ):
@@ -229,6 +229,14 @@
     first = nodes.at[0, 0, pl.ds(0, MEMBERS)]
     kept = pltpu.make_async_copy(first, coarse.at[mine], load_sem.at[6])
     kept.start()
+    loads[0].wait()
+    rank_slots(senders, slot_of, requests, picks)
+    outs = [
+        pltpu.make_async_copy(slot_of, slot_out, out_sem.at[0]),
+        pltpu.make_async_copy(picks, picks_out, out_sem.at[1]),
+    ]
+    for copy in outs:
+        copy.start()
     pl.semaphore_wait(pltpu.get_barrier_semaphore(), met)
 
     def remote(source, target, sems, at, peer):
@@ -248,6 +256,16 @@
         )
         copy.start()
         plane[near_step, y_step] = copy
+    @pl.when(lat == 0)
+    def _():
+        rim[0:5] = jnp.zeros((5, BLOCK, D), BF16)
+
+    @pl.when(lat == 3)
+    def _():
+        rim[5:10] = jnp.zeros((5, BLOCK, D), BF16)
+
+    for copy in plane.values():
+        copy.wait_send()
     halos = []
     for at, ((row, col), (r, c), (to, size)) in enumerate(HALO):
         source = nodes.at[pl.ds(0, 2), c] if r is None else nodes.at[r, pl.ds(*c)]
@@ -258,23 +276,8 @@
             copy.start()
         halos.append((row, copy))
 
-    @pl.when(lat == 0)
-    def _():
-        rim[0:5] = jnp.zeros((5, BLOCK, D), BF16)
-
-    @pl.when(lat == 3)
-    def _():
-        rim[5:10] = jnp.zeros((5, BLOCK, D), BF16)
-
-    for copy in loads:
+    for copy in loads[1:]:
         copy.wait()
-    rank_slots(senders, slot_of, requests, picks)
-    outs = [
-        pltpu.make_async_copy(slot_of, slot_out, out_sem.at[0]),
-        pltpu.make_async_copy(picks, picks_out, out_sem.at[1]),
-    ]
-    for copy in outs:
-        copy.start()
     table[0:NODES] = dot(node_rows[...], weights_v[0]).astype(BF16)
     table[NODES : 2 * NODES] = dot(node_rows[...], weights_v[1]).astype(BF16)
     core_ids = [lane_ids(CORE_BASES[at], CORE_BASES[at + 1]) for at in (0, 2, 4)]
@@ -294,8 +297,9 @@
     def rim_turn(turn, carry):
         whole = turn_of(turn)
         for at in steps_of(turn):
-            pre_v[at] += dot(hot_rows(column(slot_of[0:1, at]), rim_ids), table[:RIM])
-        pltpu.make_async_copy(pre_v.at[whole], pre.at[whole], pre_sem.at[turn]).start()
+            near_rows = dot(hot_rows(column(slot_of[0:1, at]), rim_ids), table[:RIM])
+            pre_out[at] = (pre_v[at] + near_rows).astype(BF16)
+        pltpu.make_async_copy(pre_out.at[whole], pre.at[whole], pre_sem.at[turn]).start()
         return carry
 
     def piece(step):
@@ -329,23 +333,25 @@
         rows = dot(picks[at], coarse[pl.ds(group * GROUP, GROUP)].reshape(GROUP * MEMBERS, D)).astype(BF16)
         packed[at] = dot(rows, weights_v[1]).astype(BF16)
 
+    lax.fori_loop(0, 1, own_turn, 0)
     kept.wait()
     send_far(0)
     for part in (1, 3, 2):
         send_far(part)
     hand_over(0)
-    lax.fori_loop(0, TURNS, own_turn, 0)
+    lax.fori_loop(1, TURNS, own_turn, 0)
     for row, copy in halos:
         if row:
             pl.when(reaches(lat, -row))(copy.wait_recv)
         else:
             copy.wait_recv()
     table[...] = dot(rim[...].reshape(RIM, D), weights_v[1]).astype(BF16)
+    hand_over(1)
     lax.fori_loop(0, 1, rim_turn, 0)
-    hand_over(1)
-    lax.fori_loop(1, TURNS, rim_turn, 0)
-    for step in (3, 2):
-        hand_over(step)
+    hand_over(3)
+    lax.fori_loop(1, 2, rim_turn, 0)
+    hand_over(2)
+    lax.fori_loop(2, TURNS, rim_turn, 0)
     for step in range(4):
         pack(core * 4 + step)
     for copy in passes:
@@ -356,7 +362,7 @@
     copy.start()
     for turn in range(TURNS):
         at = turn_of(turn)
-        pltpu.make_async_copy(pre_v.at[at], pre.at[at], pre_sem.at[turn]).wait()
+        pltpu.make_async_copy(pre_out.at[at], pre.at[at], pre_sem.at[turn]).wait()
     for copy in outs + [copy]:
         copy.wait()
     for row, copy in halos:
@@ -364,7 +370,7 @@
             pl.when(reaches(lat, row))(copy.wait_send)
         else:
             copy.wait_send()
-    for copy in list(plane.values()) + list(far_copies.values()) + passes:
+    for copy in list(far_copies.values()) + passes:
         copy.wait_send()
 
 
@@ -374,7 +380,7 @@
     return pl.pallas_call(
         spread_kernel,
         out_shape=(
-            jax.ShapeDtypeStruct((SLOTS, D), F32),
+            jax.ShapeDtypeStruct((SLOTS, D), BF16),
             jax.ShapeDtypeStruct((8, SLOTS), jnp.int32),
             jax.ShapeDtypeStruct((PACKED, GROUP * MEMBERS), BF16),
             jax.ShapeDtypeStruct((PACKED, D), BF16),
@@ -386,6 +392,7 @@
             pltpu.VMEM((14, BLOCK, D), BF16),
             pltpu.VMEM((SLOTS, D), BF16),
             pltpu.VMEM((SLOTS, D), F32),
+            pltpu.VMEM((SLOTS, D), BF16),
             pltpu.VMEM((3, D, D), BF16),
             pltpu.VMEM((RIM, D), BF16),
             pltpu.VMEM((PACKED, D), BF16),
@@ -406,9 +413,9 @@
 
 
 def collect_kernel(
-    far_grad, slot_in, receivers_in, pre_grad, send_in, recv_in, out,
-    pre_grad_v, own_far, paired, summed, far_in, plane_sum, plane_in, rim, rim_in, total,
-    slot_of, receivers, send_w, recv_w,
+    slot_in, receivers_in, picks_in, pre_grad, send_in, recv_in, out,
+    pre_grad_v, far_grad, paired, summed, far_in, plane_sum, plane_in, rim, rim_in, total,
+    slot_of, receivers, picks, send_w, recv_w,
     load_sem, halo_send, halo_recv, pair_send, pair_recv, far_send, far_recv, plane_send, plane_recv,
 ):
     lat, lon = places()
@@ -417,7 +424,7 @@
     partner = shifted(lat, lon, 1 - 2 * core, 0)
     loads = []
     sources = (
-        (slot_in, slot_of), (pre_grad, pre_grad_v), (far_grad.at[pl.ds(core * SAME_CORE, SAME_CORE)], own_far),
+        (slot_in, slot_of), (pre_grad, pre_grad_v), (picks_in, picks),
         (receivers_in, receivers), (recv_in, recv_w), (send_in, send_w),
     )
     for at, (source, target) in enumerate(sources):
@@ -445,23 +452,33 @@
         rim_in[3:6] = jnp.zeros((3, BLOCK, D), BF16)
         rim_in[12:14] = jnp.zeros((2, BLOCK, D), BF16)
 
+    def summed_by(ids, rows):
+        mask = jnp.broadcast_to(ids, (rows.shape[0], SLOTS)) == rows
+        return dot(onehot(mask), pre_grad_v[...])
+
+    def gathered(ids, bases):
+        return summed_by(ids, row_ids(bases))
+
+    half = PACKED // 2
+
+    def far_rows(side):
+        rows = lax.broadcasted_iota(jnp.int32, (half, 1), 0) + (EXT + side * half)
+        got = summed_by(slot_of[0:1, :], rows).astype(BF16)
+        for group in range(4):
+            wanted = picks[pl.ds(pl.multiple_of(side * half + group * LANES, LANES), LANES)]
+            block = t_dot(wanted, got[group * LANES : (group + 1) * LANES]).astype(BF16)
+            far_grad[side, group] = block.reshape(4, 4, MEMBERS, D)
+
+    for copy in loads[:3]:
+        copy.wait()
+    far_rows(1 - core)
     pl.semaphore_wait(pltpu.get_barrier_semaphore(), met)
     pairs = []
-    for step in (1, 3, 2, 0):
-        at = lax.rem(near + step, 4) * 16
-        copy = remote(
-            far_grad.at[pl.ds((1 - core) * SAME_CORE + at, 16)], paired.at[pl.ds(at, 16)], (pair_send, pair_recv), step, partner
-        )
+    for part in (1, 3, 2, 0):
+        at = lax.rem(far + part, 4)
+        copy = remote(far_grad.at[1 - core, :, at], paired.at[:, at], (pair_send, pair_recv), part, partner)
         copy.start()
-        pairs.append((step, copy))
-
-    def gathered(ids, bases):
-        rows = row_ids(bases)
-        mask = jnp.broadcast_to(ids, (rows.shape[0], SLOTS)) == rows
-        return dot(onehot(mask), pre_grad_v[...])
-
-    for copy in loads:
-        copy.wait()
+        pairs.append((part, copy))
     slots = slot_of[0:1, :]
     rim[0:5] = gathered(slots, RIM_BASES[0:5]).astype(BF16).reshape(5, BLOCK, D)
     rim[5:10] = gathered(slots, RIM_BASES[5:10]).astype(BF16).reshape(5, BLOCK, D)
@@ -476,40 +493,46 @@
         else:
             copy.start()
         halos.append((row, copy))
-
-    copies = []
-    for step, copy in pairs:
+    far_rows(core)
+
+    copies = {}
+    for part, copy in pairs:
         copy.wait_recv()
-        at = lax.rem(far + step, 4) * 16
-        for row in range(16):
-            summed[at + row] = (own_far[at + row].astype(F32) + paired[at + row].astype(F32)).astype(BF16)
-        if step:
-            sent = remote(
-                summed.at[pl.ds(at, 16)], far_in.at[step - 1], (far_send, far_recv), step - 1, device(0, 0, step)
-            )
-            sent.start()
-            copies.append(sent)
-
+        at = lax.rem(near + part, 4)
+        for step in (1, 3, 2, 0):
+            to = lax.rem(far + step, 4)
+            summed[to, at] = (far_grad[core, to, at].astype(F32) + paired[to, at].astype(F32)).astype(BF16)
+            if step:
+                slot = part * 3 + step - 1
+                copies[part, step] = remote(
+                    summed.at[to, at], far_in.at[slot], (far_send, far_recv), slot, device(0, 0, step)
+                )
+                copies[part, step].start()
+
+    for copy in loads[3:]:
+        copy.wait()
     total[...] = gathered(slots, CORE_BASES)
     got = gathered(receivers[...], tuple(range(0, NODES, BLOCK))).astype(BF16)
     out[...] = dot_t(got, recv_w[...])
 
-    for copy in copies:
-        copy.wait_recv()
     plane = []
-    for near_step, y_step in PLANE + ((0, 0),):
-        at = lax.rem(near + near_step, 4) * 4 + lax.rem(y + y_step, 4)
-        acc = summed[far * 16 + at].astype(F32)
-        for peer in range(3):
-            acc += far_in[peer, at].astype(F32)
-        if near_step or y_step:
-            plane_sum[at] = acc.astype(BF16)
-            slot = near_step * 4 + y_step - 1
-            sent = remote(
-                plane_sum.at[at], plane_in.at[slot], (plane_send, plane_recv), slot, device(y_step, near_step, 0)
-            )
-            sent.start()
-            plane.append(sent)
+    for part in (1, 3, 2, 0):
+        for step in (1, 3, 2):
+            copies[part, step].wait_recv()
+        at = lax.rem(near + part, 4)
+        for y_step in (1, 3, 2, 0):
+            y_at = lax.rem(y + y_step, 4)
+            acc = summed[far, at, y_at].astype(F32)
+            for step in range(3):
+                acc += far_in[part * 3 + step, y_at].astype(F32)
+            if part or y_step:
+                slot = part * 4 + y_step - 1
+                plane_sum[slot] = acc.astype(BF16)
+                sent = remote(
+                    plane_sum.at[slot], plane_in.at[slot], (plane_send, plane_recv), slot, device(y_step, part, 0)
+                )
+                sent.start()
+                plane.append(sent)
 
     for row, copy in halos:
         if row:
@@ -537,42 +560,42 @@
             pl.when(reaches(lat, row))(copy.wait_send)
         else:
             copy.wait_send()
-    for copy in copies + plane + [copy for _, copy in pairs]:
+    for copy in list(copies.values()) + plane + [copy for _, copy in pairs]:
         copy.wait_send()
 
 
-def collect(far_grad, slot_of, receivers, pre_grad, send_w, recv_w):
-    vmem = pl.BlockSpec(memory_space=pltpu.VMEM)
+def collect(slot_of, receivers, picks, pre_grad, send_w, recv_w):
     hbm = pl.BlockSpec(memory_space=pl.ANY)
     dma = pltpu.SemaphoreType.DMA
     return pl.pallas_call(
         collect_kernel,
         out_shape=jax.ShapeDtypeStruct((NODES, D), F32),
         in_specs=[hbm] * 6,
-        out_specs=vmem,
+        out_specs=pl.BlockSpec(memory_space=pltpu.VMEM),
         scratch_shapes=[
             pltpu.VMEM((SLOTS, D), BF16),
-            pltpu.VMEM((SAME_CORE, MEMBERS, D), BF16),
-            pltpu.VMEM((SAME_CORE, MEMBERS, D), BF16),
-            pltpu.VMEM((SAME_CORE, MEMBERS, D), BF16),
-            pltpu.VMEM((3, 16, MEMBERS, D), BF16),
-            pltpu.VMEM((16, MEMBERS, D), BF16),
+            pltpu.VMEM((2, 4, 4, 4, MEMBERS, D), BF16),
+            pltpu.VMEM((4, 4, 4, MEMBERS, D), BF16),
+            pltpu.VMEM((4, 4, 4, MEMBERS, D), BF16),
+            pltpu.VMEM((12, 4, MEMBERS, D), BF16),
+            pltpu.VMEM((15, MEMBERS, D), BF16),
             pltpu.VMEM((15, MEMBERS, D), BF16),
             pltpu.VMEM((14, BLOCK, D), BF16),
             pltpu.VMEM((14, BLOCK, D), BF16),
             pltpu.VMEM((NODES, D), F32),
             pltpu.VMEM((8, SLOTS), jnp.int32),
             pltpu.VMEM((1, SLOTS), jnp.int32),
+            pltpu.VMEM((PACKED, GROUP * MEMBERS), BF16),
             pltpu.VMEM((D, D), BF16),
             pltpu.VMEM((D, D), BF16),
             dma((6,)), dma((8,)), dma((8,)), dma((4,)), dma((4,)),
-            dma((3,)), dma((3,)), dma((15,)), dma((15,)),
+            dma((12,)), dma((12,)), dma((15,)), dma((15,)),
         ],
         compiler_params=pltpu.CompilerParams(
             collective_id=1, has_side_effects=True, vmem_limit_bytes=VMEM_BYTES
         ),
         name="collect",
-    )(far_grad, slot_of, receivers, pre_grad, send_w, recv_w)
+    )(slot_of, receivers, picks, pre_grad, send_w, recv_w)
 
 
 def centered(weight):
@@ -591,11 +614,12 @@
 
 
 def layer_kernel(
-    count, slot_of, receivers, picks, table, nodes, node_up, pre, edges, edge_up,
-    out_w, self_w, node_w, aggr_w, node_out, edge_gain, node_gain,
-    node_new, edge_new, node_grad, edge_grad, pre_grad, far_grad,
-    pre_v, edges_v, up_v, new_v, grad_v, packed, normed_v, slope_v, rstd_v, pre_grad_v, aggr, aggr_grad, out_c,
-    pre_sem, edges_sem, up_sem, new_sem, grad_sem, pre_grad_sem,
+    count, edge_gain, node_gain, slot_in, receivers_in, table_in, nodes_in, node_up_in, pre, edges, edge_up,
+    out_in, self_in, node_in, aggr_in, node_out_in,
+    node_new_out, edge_new, node_grad_out, edge_grad, pre_grad,
+    pre_v, edges_v, up_v, new_v, grad_v, normed_v, slope_v, rstd_v, pre_grad_v, aggr, aggr_grad, out_c,
+    slot_of, receivers, table, nodes, node_up, out_w, self_w, node_w, aggr_w, node_out, node_new, node_grad,
+    load_sem, pre_sem, edges_sem, up_sem, new_sem, grad_sem, pre_grad_sem,
 ):
     def loaded(turn):
         at = turn_of(turn)
@@ -608,11 +632,23 @@
         at = turn_of(turn)
         return pltpu.make_async_copy(edge_up.at[at], up_v.at[at], up_sem.at[turn])
 
+    sources = (
+        (out_in, out_w), (slot_in, slot_of), (table_in, table), (receivers_in, receivers),
+        (nodes_in, nodes), (node_up_in, node_up), (node_in, node_w), (aggr_in, aggr_w), (node_out_in, node_out),
+        (self_in, self_w),
+    )
+    loads = [pltpu.make_async_copy(source, target, load_sem.at[at]) for at, (source, target) in enumerate(sources)]
+    for copy in loads[:4]:
+        copy.start()
     for turn in range(TURNS):
         for copy in loaded(turn):
             copy.start()
+    for copy in loads[4:]:
+        copy.start()
     for turn in range(TURNS):
         raised(turn).start()
+    for copy in loads[:4]:
+        copy.wait()
 
     out_c[...] = centered(out_w)
     node_row = lax.broadcasted_iota(jnp.int32, (NODES, WIDE), 0)
@@ -659,6 +695,8 @@
 
     lax.fori_loop(0, TURNS, forward, 0)
 
+    for copy in loads[4:]:
+        copy.wait()
     node_rows = nodes[...]
     node_pre = dot(node_rows, node_w[...]) + dot(aggr[...].astype(BF16), aggr_w[...])
     gate = sigmoid(node_pre)
@@ -671,6 +709,12 @@
     node_pre_grad = (dot_t(hidden_grad, node_out[...]) * slope).astype(BF16)
     node_grad[...] = up + dot_t(node_pre_grad, node_w[...])
     aggr_grad[...] = dot_t(node_pre_grad, aggr_w[...]).astype(BF16)
+    outs = (
+        pltpu.make_async_copy(node_new, node_new_out, load_sem.at[10]),
+        pltpu.make_async_copy(node_grad, node_grad_out, load_sem.at[11]),
+    )
+    for copy in outs:
+        copy.start()
 
     def backward(turn, carry):
         raised(turn).wait()
@@ -689,26 +733,15 @@
 
     lax.fori_loop(0, TURNS, backward, 0)
 
-    def far_step(step, carry):
-        base = EXT + step * STEP
-        mask = jnp.broadcast_to(slot_of[0:1, :], (STEP, SLOTS)) == lax.broadcasted_iota(jnp.int32, (STEP, SLOTS), 0) + base
-        packed[rows_of(step)] = dot(onehot(mask), pre_grad_v[...]).astype(BF16)
-        return carry
-
-    lax.fori_loop(0, PACKED // STEP, far_step, 0)
-    for group in range(GROUPS):
-        at, span = group * LANES, GROUP * MEMBERS
-        far_grad[group * span : (group + 1) * span] = t_dot(
-            picks[at : at + LANES], packed[at : at + LANES]
-        ).astype(BF16)
-
+    for copy in outs:
+        copy.wait()
     for turn in range(TURNS):
         stored(turn).wait()
         for copy in returned(turn):
             copy.wait()
 
 
-def layer(count, slot_of, receivers, picks, table, nodes, node_up, pre, edges, edge_up, weights, gains):
+def layer(count, edge_gain, node_gain, *rows):
     vmem = pl.BlockSpec(memory_space=pltpu.VMEM)
     smem = pl.BlockSpec(memory_space=pltpu.SMEM)
     hbm = pl.BlockSpec(memory_space=pl.ANY)
@@ -721,17 +754,15 @@
             jax.ShapeDtypeStruct((NODES, D), F32),
             jax.ShapeDtypeStruct((SLOTS, D), F32),
             jax.ShapeDtypeStruct((SLOTS, D), BF16),
-            jax.ShapeDtypeStruct((COARSE, D), BF16),
         ),
-        in_specs=[smem] + [vmem] * 6 + [hbm] * 3 + [vmem] * 7,
-        out_specs=(vmem, hbm, vmem, hbm, hbm, vmem),
+        in_specs=[smem, vmem, vmem] + [hbm] * len(rows),
+        out_specs=(hbm,) * 5,
         scratch_shapes=[
+            pltpu.VMEM((SLOTS, D), BF16),
+            pltpu.VMEM((SLOTS, D), BF16),
+            pltpu.VMEM((SLOTS, D), BF16),
+            pltpu.VMEM((SLOTS, D), BF16),
             pltpu.VMEM((SLOTS, D), F32),
-            pltpu.VMEM((SLOTS, D), BF16),
-            pltpu.VMEM((SLOTS, D), BF16),
-            pltpu.VMEM((SLOTS, D), BF16),
-            pltpu.VMEM((SLOTS, D), F32),
-            pltpu.VMEM((PACKED, D), BF16),
             pltpu.VMEM((SLOTS, D), BF16),
             pltpu.VMEM((SLOTS, D), BF16),
             pltpu.VMEM((SLOTS, LANES), F32),
@@ -739,11 +770,19 @@
             pltpu.VMEM((NODES, D), F32),
             pltpu.VMEM((NODES, D), BF16),
             pltpu.VMEM((D, D), BF16),
+            pltpu.VMEM((8, SLOTS), jnp.int32),
+            pltpu.VMEM((1, SLOTS), jnp.int32),
+            pltpu.VMEM((PACKED, D), BF16),
+            pltpu.VMEM((NODES, D), BF16),
+            pltpu.VMEM((NODES, D), BF16),
         ]
+        + [pltpu.VMEM((D, D), BF16)] * 5
+        + [pltpu.VMEM((NODES, D), BF16), pltpu.VMEM((NODES, D), F32)]
+        + [dma((12,))]
         + [dma((TURNS,))] * 6,
         compiler_params=pltpu.CompilerParams(vmem_limit_bytes=VMEM_BYTES),
         name="layer",
-    )(count, slot_of, receivers, picks, table, nodes, node_up, pre, edges, edge_up, *weights, *gains)
+    )(count, edge_gain, node_gain, *rows)
 
 
 def body(
@@ -771,21 +810,25 @@
     pre, slot_of, picks, table = spread(
         node_latents, senders.reshape(1, SLOTS), to, node_rows, edges, edge_self_w, edge_send_w, edge_recv_w
     )
-    node_new, edge_new, node_grad, edge_grad, pre_grad, far_grad = layer(
+    node_new, edge_new, node_grad, edge_grad, pre_grad = layer(
         edge_count,
+        edge_gain.reshape(1, D),
+        node_gain.reshape(1, D),
         slot_of,
         to,
-        picks,
         table,
         node_rows,
         node_upstream.reshape(NODES, D),
         pre,
         edges,
         edge_upstream.reshape(SLOTS, D),
-        (edge_out_w, edge_self_w, node_self_w, node_aggr_w, node_out_w),
-        (edge_gain.reshape(1, D), node_gain.reshape(1, D)),
+        edge_out_w,
+        edge_self_w,
+        node_self_w,
+        node_aggr_w,
+        node_out_w,
     )
-    returned = collect(far_grad.reshape(OWNERS, MEMBERS, D), slot_of, to, pre_grad, edge_send_w, edge_recv_w)
+    returned = collect(slot_of, to, picks, pre_grad, edge_send_w, edge_recv_w)
     return (
         node_new.reshape(grid),
         edge_new.reshape(edge_latents.shape),

time: 95.6 us -> 88.1 us (0.922)
  Pallas kernels: 92 us -> 84.4 us
    pallas_call x1, Pallas kernels: 27.8 us -> 22 us  [layer(): pl.pallas_call(layer_kernel, out_shape=(jax.ShapeDtypeStruct((NODES, D),...]
    pallas_call x1, Pallas kernels: 34.9 us -> 33.4 us  [spread(): pl.pallas_call(spread_kernel, out_shape=(jax.ShapeDtypeStruct((SLOTS, D),...]
where the time goes in v4:
time: 88.1 us; the launch traced here: 87.9 us
  Pallas kernels  84.4 us (96%)
  other arithmetic  2.15 us (2%)
  between operations  1.32 us (1%)
    pallas_call x1, Pallas kernels, spread(): pl.pallas_call(spread_kernel, out_shape=(jax.ShapeDtypeStruct((SLOTS, D),...  33.4 us
    pallas_call x1, Pallas kernels, collect(): pl.pallas_call(collect_kernel, out_shape=jax.ShapeDtypeStruct((NODES, D),...  29.1 us
    pallas_call x1, Pallas kernels, layer(): pl.pallas_call(layer_kernel, out_shape=(jax.ShapeDtypeStruct((NODES, D),...  22 us
    add x1, other arithmetic, body(): node_grad + returned  2.15 us

profile of v4, /device:TPU:1, one launch (start us, length us, event | category | flops | bytes accessed | tf_op | source)
XLA Modules:
  0.0 87.9 jit_solution(9845741942131595254)
XLA Ops:
  1.3 33.4 %spread.1 = (bf16[3072,512]{1,0:T(8,128)(2,1)}, s32[8,3072]{1,0:T(8,128)}, bf16[1024,256]{1,0:T(8,128)(2,1)}, bf16[1024,512]{1,0:T(8,128)(2,1)}) custom-call(bf16[2,3,64,512]{3,2,1,0:T(8,128)(2,1)} %nodes.1, s32[1,3072]{1,0:T(1,128)} %bitcast.22, s32[1,3072]{1,0:T(1,128)} %bitcast.19, bf16[384,512]{1,0:T(8,128)(2,1)} %bitcast.14, ...), custom_call_target="tpu_custom_call" | custom-call | tf_op jit(solution)/shard_map/spread/pallas_call | solution.py:380
  34.7 22.0 %layer.1 = (bf16[384,512]{1,0:T(8,128)(2,1)}, bf16[3072,512]{1,0:T(8,128)(2,1)}, f32[384,512]{1,0:T(8,128)}, f32[3072,512]{1,0:T(8,128)}, bf16[3072,512]{1,0:T(8,128)(2,1)}) custom-call(s32[1,1]{1,0:T(1,128)S(6)} %copy.20.count, f32[1,512]{1,0:T(1,128)} %bitcast.23, f32[1,512]{1,0:T(1,128)} %bitcast.24, s32[8,3072]{1,0:T(8,128)} %get-tuple-element.13.slot_in, ...), custom_call_target="tpu_custom_call" | custom-call | tf_op jit(solution)/shard_map/layer/pallas_call | solution.py:749
  56.6 0.0 copy-start
  56.6 29.1 %collect.1 = f32[384,512]{1,0:T(8,128)} custom-call(s32[8,3072]{1,0:T(8,128)} %get-tuple-element.13.slot_in, s32[1,3072]{1,0:T(1,128)} %bitcast.21, bf16[1024,256]{1,0:T(8,128)(2,1)} %get-tuple-element.19.picks_in, bf16[3072,512]{1,0:T(8,128)(2,1)} %get-tuple-element.20.pre_grad, bf16[512,512]{1,0:T(8,128)(2,1)} %send_in.1, bf16[512,512]{1,0:T(8,128)(2,1)} %recv_in.1), custom_call_target="tpu_custom_call" | custom-call | tf_op jit(solution)/shard_map/collect/pallas_call | solution.py:570
  85.7 0.0 copy-done
  85.7 2.2 %add.3 = f32[384,512]{1,0:T(8,128)} add(f32[384,512]{1,0:T(8,128)S(1)} %copy-done, f32[384,512]{1,0:T(8,128)} %collect.1) | non-fusion elementwise | flops 196608 | bytes 2359296 | tf_op jit(solution)/shard_map/add | solution.py:835
Async XLA Ops:
  56.6 29.1 %copy-start = (f32[384,512]{1,0:T(8,128)S(1)}, f32[384,512]{1,0:T(8,128)}, u32[]{:S(2)}) copy-start(f32[384,512]{1,0:T(8,128)} %get-tuple-element.18) | copy-start | bytes 2359300

commit v5 on v4

--- a/solution.py
+++ b/solution.py
@@ -31,6 +31,7 @@
 LONS = 32
 SAME_CORE = 64
 RIM = 14 * BLOCK
+SIDES = 10 * BLOCK
 VMEM_BYTES = 60 * 1024 * 1024
 
 
@@ -102,10 +103,10 @@
 RIM_BASES = (0, 64, 128, 192, 256, 960, 1024, 1088, 1152, 1216, 320, 640, 576, 896)
 CORE_BASES = (384, 448, 512, 704, 768, 832)
 HALO = (
+    ((0, -1), (None, 0), (12, 2)),
+    ((0, 1), (None, 2), (10, 2)),
     ((-1, 0), (0, (0, 3)), (6, 3)),
     ((1, 0), (1, (0, 3)), (1, 3)),
-    ((0, -1), (None, 0), (12, 2)),
-    ((0, 1), (None, 2), (10, 2)),
     ((-1, -1), (0, (0, 1)), (9, 1)),
     ((-1, 1), (0, (2, 1)), (5, 1)),
     ((1, -1), (1, (0, 1)), (4, 1)),
@@ -206,7 +207,7 @@
     pre, slot_out, picks_out, table_out,
     coarse, rim, edges_v, pre_v, pre_out, weights_v, table, packed, requests, senders, receivers, node_rows, slot_of, picks,
     load_sem, out_sem, edges_sem, pre_sem, halo_send, halo_recv,
-    plane_send, plane_recv, far_send, far_recv, pass_send, pass_recv,
+    plane_send, plane_recv, far_send, far_recv, pass_send, pass_recv, corner_send, corner_recv,
 ):
     lat, lon = places()
     core, y, near, far, device = rings(lat, lon)
@@ -270,11 +271,14 @@
     for at, ((row, col), (r, c), (to, size)) in enumerate(HALO):
         source = nodes.at[pl.ds(0, 2), c] if r is None else nodes.at[r, pl.ds(*c)]
         copy = remote(source, rim.at[pl.ds(to, size)], (halo_send, halo_recv), at, shifted(lat, lon, row, col))
-        if row:
-            pl.when(reaches(lat, row))(copy.start)
+        if row and col:
+            sends, gets = lat == (2 if row < 0 else 1), lat == (1 if row < 0 else 2)
+        elif row:
+            sends, gets = reaches(lat, row), reaches(lat, -row)
         else:
-            copy.start()
-        halos.append((row, copy))
+            sends = gets = None
+        copy.start() if sends is None else pl.when(sends)(copy.start)
+        halos.append((sends, gets, copy))
 
     for copy in loads[1:]:
         copy.wait()
@@ -294,10 +298,15 @@
             pre_v[at] = dot(edges_v[at], weights_v[2]) + dot(hot, table[: 2 * NODES])
         return carry
 
+    def side_turn(turn, carry):
+        for at in steps_of(turn):
+            pre_v[at] += dot(hot_rows(column(slot_of[0:1, at]), rim_ids[5:]), table[SIDES:RIM])
+        return carry
+
     def rim_turn(turn, carry):
         whole = turn_of(turn)
         for at in steps_of(turn):
-            near_rows = dot(hot_rows(column(slot_of[0:1, at]), rim_ids), table[:RIM])
+            near_rows = dot(hot_rows(column(slot_of[0:1, at]), rim_ids[:5]), table[:SIDES])
             pre_out[at] = (pre_v[at] + near_rows).astype(BF16)
         pltpu.make_async_copy(pre_out.at[whole], pre.at[whole], pre_sem.at[turn]).start()
         return carry
@@ -340,12 +349,22 @@
         send_far(part)
     hand_over(0)
     lax.fori_loop(1, TURNS, own_turn, 0)
-    for row, copy in halos:
-        if row:
-            pl.when(reaches(lat, -row))(copy.wait_recv)
-        else:
-            copy.wait_recv()
-    table[...] = dot(rim[...].reshape(RIM, D), weights_v[1]).astype(BF16)
+    corners = []
+    for _, _, copy in halos[:2]:
+        copy.wait_recv()
+    for at, (column_at, row_at) in enumerate(((11, 0), (13, 4))):
+        copy = remote(
+            rim.at[column_at - core], rim.at[row_at + 5 * core], (corner_send, corner_recv), at, partner
+        )
+        copy.start()
+        corners.append(copy)
+    table[SIDES:RIM] = dot(rim[10:14].reshape(4 * BLOCK, D), weights_v[1]).astype(BF16)
+    lax.fori_loop(0, TURNS, side_turn, 0)
+    for copy in corners:
+        copy.wait_recv()
+    for _, gets, copy in halos[2:]:
+        pl.when(gets)(copy.wait_recv)
+    table[:SIDES] = dot(rim[:10].reshape(SIDES, D), weights_v[1]).astype(BF16)
     hand_over(1)
     lax.fori_loop(0, 1, rim_turn, 0)
     hand_over(3)
@@ -365,12 +384,9 @@
         pltpu.make_async_copy(pre_out.at[at], pre.at[at], pre_sem.at[turn]).wait()
     for copy in outs + [copy]:
         copy.wait()
-    for row, copy in halos:
-        if row:
-            pl.when(reaches(lat, row))(copy.wait_send)
-        else:
-            copy.wait_send()
-    for copy in list(far_copies.values()) + passes:
+    for sends, _, copy in halos:
+        copy.wait_send() if sends is None else pl.when(sends)(copy.wait_send)
+    for copy in list(far_copies.values()) + passes + corners:
         copy.wait_send()
 
 
@@ -403,7 +419,7 @@
             pltpu.VMEM((8, SLOTS), jnp.int32),
             pltpu.VMEM((PACKED, GROUP * MEMBERS), BF16),
             dma((7,)), dma((3,)), dma((TURNS,)), dma((TURNS,)), dma((8,)), dma((8,)),
-            dma((16,)), dma((16,)), dma((12,)), dma((12,)), dma((4,)), dma((4,)),
+            dma((16,)), dma((16,)), dma((12,)), dma((12,)), dma((4,)), dma((4,)), dma((2,)), dma((2,)),
         ],
         compiler_params=pltpu.CompilerParams(
             collective_id=0, has_side_effects=True, vmem_limit_bytes=VMEM_BYTES
@@ -471,18 +487,11 @@
 
     for copy in loads[:3]:
         copy.wait()
-    far_rows(1 - core)
-    pl.semaphore_wait(pltpu.get_barrier_semaphore(), met)
-    pairs = []
-    for part in (1, 3, 2, 0):
-        at = lax.rem(far + part, 4)
-        copy = remote(far_grad.at[1 - core, :, at], paired.at[:, at], (pair_send, pair_recv), part, partner)
-        copy.start()
-        pairs.append((part, copy))
     slots = slot_of[0:1, :]
     rim[0:5] = gathered(slots, RIM_BASES[0:5]).astype(BF16).reshape(5, BLOCK, D)
     rim[5:10] = gathered(slots, RIM_BASES[5:10]).astype(BF16).reshape(5, BLOCK, D)
     rim[10:14] = gathered(slots, RIM_BASES[10:14]).astype(BF16).reshape(4, BLOCK, D)
+    pl.semaphore_wait(pltpu.get_barrier_semaphore(), met)
     halos = []
     for at, ((row, col), (start, size), (to, _)) in enumerate(BACK):
         copy = remote(
@@ -493,6 +502,13 @@
         else:
             copy.start()
         halos.append((row, copy))
+    far_rows(1 - core)
+    pairs = []
+    for part in (1, 3, 2, 0):
+        at = lax.rem(far + part, 4)
+        copy = remote(far_grad.at[1 - core, :, at], paired.at[:, at], (pair_send, pair_recv), part, partner)
+        copy.start()
+        pairs.append((part, copy))
     far_rows(core)
 
     copies = {}

time: 88.1 us -> 85.2 us (0.967)
  Pallas kernels: 84.4 us -> 81.6 us
    pallas_call x1, Pallas kernels: 33.4 us -> 31.5 us  [spread(): pl.pallas_call(spread_kernel, out_shape=(jax.ShapeDtypeStruct((SLOTS, D),...]
    pallas_call x1, Pallas kernels: 29.1 us -> 28.1 us  [collect(): pl.pallas_call(collect_kernel, out_shape=jax.ShapeDtypeStruct((NODES, D),...]
where the time goes in v5:
time: 85.2 us; the launch traced here: 85 us
  Pallas kernels  81.6 us (96%)
  other arithmetic  2.15 us (3%)
  between operations  1.32 us (2%)
    pallas_call x1, Pallas kernels, spread(): pl.pallas_call(spread_kernel, out_shape=(jax.ShapeDtypeStruct((SLOTS, D),...  31.5 us
    pallas_call x1, Pallas kernels, collect(): pl.pallas_call(collect_kernel, out_shape=jax.ShapeDtypeStruct((NODES, D),...  28.1 us
    pallas_call x1, Pallas kernels, layer(): pl.pallas_call(layer_kernel, out_shape=(jax.ShapeDtypeStruct((NODES, D),...  22 us
    add x1, other arithmetic, body(): node_grad + returned  2.15 us

profile of v5, /device:TPU:1, one launch (start us, length us, event | category | flops | bytes accessed | tf_op | source)
XLA Modules:
  0.0 85.0 jit_solution(6915163063177812124)
XLA Ops:
  1.3 31.5 %spread.1 = (bf16[3072,512]{1,0:T(8,128)(2,1)}, s32[8,3072]{1,0:T(8,128)}, bf16[1024,256]{1,0:T(8,128)(2,1)}, bf16[1024,512]{1,0:T(8,128)(2,1)}) custom-call(bf16[2,3,64,512]{3,2,1,0:T(8,128)(2,1)} %nodes.1, s32[1,3072]{1,0:T(1,128)} %bitcast.22, s32[1,3072]{1,0:T(1,128)} %bitcast.19, bf16[384,512]{1,0:T(8,128)(2,1)} %bitcast.14, ...), custom_call_target="tpu_custom_call" | custom-call | tf_op jit(solution)/shard_map/spread/pallas_call | solution.py:396
  32.8 22.0 %layer.1 = (bf16[384,512]{1,0:T(8,128)(2,1)}, bf16[3072,512]{1,0:T(8,128)(2,1)}, f32[384,512]{1,0:T(8,128)}, f32[3072,512]{1,0:T(8,128)}, bf16[3072,512]{1,0:T(8,128)(2,1)}) custom-call(s32[1,1]{1,0:T(1,128)S(6)} %copy.20.count, f32[1,512]{1,0:T(1,128)} %bitcast.23, f32[1,512]{1,0:T(1,128)} %bitcast.24, s32[8,3072]{1,0:T(8,128)} %get-tuple-element.13.slot_in, ...), custom_call_target="tpu_custom_call" | custom-call | tf_op jit(solution)/shard_map/layer/pallas_call | solution.py:765
  54.8 0.0 copy-start
  54.8 28.1 %collect.1 = f32[384,512]{1,0:T(8,128)} custom-call(s32[8,3072]{1,0:T(8,128)} %get-tuple-element.13.slot_in, s32[1,3072]{1,0:T(1,128)} %bitcast.21, bf16[1024,256]{1,0:T(8,128)(2,1)} %get-tuple-element.19.picks_in, bf16[3072,512]{1,0:T(8,128)(2,1)} %get-tuple-element.20.pre_grad, bf16[512,512]{1,0:T(8,128)(2,1)} %send_in.1, bf16[512,512]{1,0:T(8,128)(2,1)} %recv_in.1), custom_call_target="tpu_custom_call" | custom-call | tf_op jit(solution)/shard_map/collect/pallas_call | solution.py:586
  82.9 0.0 copy-done
  82.9 2.2 %add.3 = f32[384,512]{1,0:T(8,128)} add(f32[384,512]{1,0:T(8,128)S(1)} %copy-done, f32[384,512]{1,0:T(8,128)} %collect.1) | non-fusion elementwise | flops 196608 | bytes 2359296 | tf_op jit(solution)/shard_map/add | solution.py:851
Async XLA Ops:
  54.8 28.1 %copy-start = (f32[384,512]{1,0:T(8,128)S(1)}, f32[384,512]{1,0:T(8,128)}, u32[]{:S(2)}) copy-start(f32[384,512]{1,0:T(8,128)} %get-tuple-element.18) | copy-start | bytes 2359300

commit v6 on v5

--- a/solution.py
+++ b/solution.py
@@ -221,23 +221,12 @@
         copy = pltpu.make_async_copy(source, target, load_sem.at[at])
         copy.start()
         loads.append(copy)
-    for turn in range(TURNS):
-        at = turn_of(turn)
-        pltpu.make_async_copy(edges.at[at], edges_v.at[at], edges_sem.at[turn]).start()
 
     base = core * SAME_CORE
     mine = base + far * 16 + near * 4 + y
     first = nodes.at[0, 0, pl.ds(0, MEMBERS)]
     kept = pltpu.make_async_copy(first, coarse.at[mine], load_sem.at[6])
     kept.start()
-    loads[0].wait()
-    rank_slots(senders, slot_of, requests, picks)
-    outs = [
-        pltpu.make_async_copy(slot_of, slot_out, out_sem.at[0]),
-        pltpu.make_async_copy(picks, picks_out, out_sem.at[1]),
-    ]
-    for copy in outs:
-        copy.start()
     pl.semaphore_wait(pltpu.get_barrier_semaphore(), met)
 
     def remote(source, target, sems, at, peer):
@@ -257,6 +246,19 @@
         )
         copy.start()
         plane[near_step, y_step] = copy
+
+    for turn in range(TURNS):
+        at = turn_of(turn)
+        pltpu.make_async_copy(edges.at[at], edges_v.at[at], edges_sem.at[turn]).start()
+
+    loads[0].wait()
+    rank_slots(senders, slot_of, requests, picks)
+    outs = [
+        pltpu.make_async_copy(slot_of, slot_out, out_sem.at[0]),
+        pltpu.make_async_copy(picks, picks_out, out_sem.at[1]),
+    ]
+    for copy in outs:
+        copy.start()
     @pl.when(lat == 0)
     def _():
         rim[0:5] = jnp.zeros((5, BLOCK, D), BF16)
@@ -429,8 +431,8 @@
 
 
 def collect_kernel(
-    slot_in, receivers_in, picks_in, pre_grad, send_in, recv_in, out,
-    pre_grad_v, far_grad, paired, summed, far_in, plane_sum, plane_in, rim, rim_in, total,
+    slot_in, receivers_in, picks_in, pre_grad, send_in, recv_in, returned,
+    out, pre_grad_v, far_grad, paired, summed, far_in, plane_sum, plane_in, rim, rim_in, total,
     slot_of, receivers, picks, send_w, recv_w,
     load_sem, halo_send, halo_recv, pair_send, pair_recv, far_send, far_recv, plane_send, plane_recv,
 ):
@@ -564,6 +566,8 @@
     for at, block in ((0, 6), (3, 7), (2, 8), (5, 9), (0, 10), (2, 11), (3, 12), (5, 13)):
         add(at, block)
     out[BLOCK:] += dot_t(total[BLOCK:].astype(BF16), send_w[...])
+    rest = pltpu.make_async_copy(out.at[pl.ds(BLOCK, NODES - BLOCK)], returned.at[pl.ds(BLOCK, NODES - BLOCK)], load_sem.at[6])
+    rest.start()
 
     for copy in plane:
         copy.wait_recv()
@@ -571,6 +575,8 @@
         acc += plane_in[slot].astype(F32)
     total[:MEMBERS] += acc
     out[:BLOCK] += dot_t(total[:BLOCK].astype(BF16), send_w[...])
+    head = pltpu.make_async_copy(out.at[pl.ds(0, BLOCK)], returned.at[pl.ds(0, BLOCK)], load_sem.at[7])
+    head.start()
     for row, copy in halos:
         if row:
             pl.when(reaches(lat, row))(copy.wait_send)
@@ -578,6 +584,8 @@
             copy.wait_send()
     for copy in list(copies.values()) + plane + [copy for _, copy in pairs]:
         copy.wait_send()
+    rest.wait()
+    head.wait()
 
 
 def collect(slot_of, receivers, picks, pre_grad, send_w, recv_w):
@@ -587,8 +595,9 @@
         collect_kernel,
         out_shape=jax.ShapeDtypeStruct((NODES, D), F32),
         in_specs=[hbm] * 6,
-        out_specs=pl.BlockSpec(memory_space=pltpu.VMEM),
+        out_specs=hbm,
         scratch_shapes=[
+            pltpu.VMEM((NODES, D), F32),
             pltpu.VMEM((SLOTS, D), BF16),
             pltpu.VMEM((2, 4, 4, 4, MEMBERS, D), BF16),
             pltpu.VMEM((4, 4, 4, MEMBERS, D), BF16),
@@ -604,7 +613,7 @@
             pltpu.VMEM((PACKED, GROUP * MEMBERS), BF16),
             pltpu.VMEM((D, D), BF16),
             pltpu.VMEM((D, D), BF16),
-            dma((6,)), dma((8,)), dma((8,)), dma((4,)), dma((4,)),
+            dma((8,)), dma((8,)), dma((8,)), dma((4,)), dma((4,)),
             dma((12,)), dma((12,)), dma((15,)), dma((15,)),
         ],
         compiler_params=pltpu.CompilerParams(

time: 85.2 us -> 84.9 us (level)
  no operation moved by 1% of the time
where the time goes in v6:
time: 84.9 us; the launch traced here: 84.7 us
  Pallas kernels  81.3 us (96%)
  other arithmetic  2.15 us (3%)
  between operations  1.32 us (2%)
    pallas_call x1, Pallas kernels, spread(): pl.pallas_call(spread_kernel, out_shape=(jax.ShapeDtypeStruct((SLOTS, D),...  31.2 us
    pallas_call x1, Pallas kernels, collect(): pl.pallas_call(collect_kernel, out_shape=jax.ShapeDtypeStruct((NODES, D),...  28.1 us
    pallas_call x1, Pallas kernels, layer(): pl.pallas_call(layer_kernel, out_shape=(jax.ShapeDtypeStruct((NODES, D),...  22 us
    add x1, other arithmetic, body(): node_grad + returned  2.15 us

profile of v6, /device:TPU:1, one launch (start us, length us, event | category | flops | bytes accessed | tf_op | source)
XLA Modules:
  0.0 84.7 jit_solution(17132297536147409114)
XLA Ops:
  1.3 31.2 %spread.1 = (bf16[3072,512]{1,0:T(8,128)(2,1)}, s32[8,3072]{1,0:T(8,128)}, bf16[1024,256]{1,0:T(8,128)(2,1)}, bf16[1024,512]{1,0:T(8,128)(2,1)}) custom-call(bf16[2,3,64,512]{3,2,1,0:T(8,128)(2,1)} %nodes.1, s32[1,3072]{1,0:T(1,128)} %bitcast.22, s32[1,3072]{1,0:T(1,128)} %bitcast.19, bf16[384,512]{1,0:T(8,128)(2,1)} %bitcast.14, ...), custom_call_target="tpu_custom_call" | custom-call | tf_op jit(solution)/shard_map/spread/pallas_call | solution.py:398
  32.5 22.0 %layer.1 = (bf16[384,512]{1,0:T(8,128)(2,1)}, bf16[3072,512]{1,0:T(8,128)(2,1)}, f32[384,512]{1,0:T(8,128)}, f32[3072,512]{1,0:T(8,128)}, bf16[3072,512]{1,0:T(8,128)(2,1)}) custom-call(s32[1,1]{1,0:T(1,128)S(6)} %copy.20.count, f32[1,512]{1,0:T(1,128)} %bitcast.23, f32[1,512]{1,0:T(1,128)} %bitcast.24, s32[8,3072]{1,0:T(8,128)} %get-tuple-element.13.slot_in, ...), custom_call_target="tpu_custom_call" | custom-call | tf_op jit(solution)/shard_map/layer/pallas_call | solution.py:774
  54.5 0.0 copy-start
  54.5 28.1 %collect.1 = f32[384,512]{1,0:T(8,128)} custom-call(s32[8,3072]{1,0:T(8,128)} %get-tuple-element.13.slot_in, s32[1,3072]{1,0:T(1,128)} %bitcast.21, bf16[1024,256]{1,0:T(8,128)(2,1)} %get-tuple-element.19.picks_in, bf16[3072,512]{1,0:T(8,128)(2,1)} %get-tuple-element.20.pre_grad, bf16[512,512]{1,0:T(8,128)(2,1)} %send_in.1, bf16[512,512]{1,0:T(8,128)(2,1)} %recv_in.1), custom_call_target="tpu_custom_call" | custom-call | tf_op jit(solution)/shard_map/collect/pallas_call | solution.py:594
  82.6 0.0 copy-done
  82.6 2.2 %add.3 = f32[384,512]{1,0:T(8,128)} add(f32[384,512]{1,0:T(8,128)S(1)} %copy-done, f32[384,512]{1,0:T(8,128)} %collect.1) | non-fusion elementwise | flops 196608 | bytes 2359296 | tf_op jit(solution)/shard_map/add | solution.py:860
Async XLA Ops:
  54.5 28.1 %copy-start = (f32[384,512]{1,0:T(8,128)S(1)}, f32[384,512]{1,0:T(8,128)}, u32[]{:S(2)}) copy-start(f32[384,512]{1,0:T(8,128)} %get-tuple-element.18) | copy-start | bytes 2359300
